TPU v7x, 128 devices: a whole 4x4x4 slice. The times are simulated.
128 devices in a mesh: lat: 4 (over z), lon: 32 (over y, x, core).
Axes of the slice: x: 4, y: 4, z: 4, core: 2. Of those that a mesh axis runs over, the one named last changes fastest.
Arguments:
- observations: float32 [64, 96, 4096], P('lon', 'lat'), may hold values from 0 to 83
- aux_state: float32 [64, 96, 4096], P('lon', 'lat'), may hold values from -4 to 4
- dual_state: float32 [64, 96, 4096], P('lon', 'lat'), may hold values from -4 to 4
- predictors: float32 [64, 512], replicated, may hold values from -0.25 to 0.25
- inverse_gram: float32 [512, 512], replicated, as said below
Outputs:
- coefficients: float32 [512, 96, 4096], P(None, 'lat', 'lon')
- aux_next: float32 [64, 96, 4096], P('lon', 'lat')
- dual_next: float32 [64, 96, 4096], P('lon', 'lat')
- primal_norm: float32 [], replicated
- dual_norm: float32 [], replicated
Inputs may be any that keep to these rules, and one draw needn't show every extreme that they name: `inverse_gram`: symmetric.
All inputs are finite; a program needn't handle non-finite values.
Results may differ from a plain program's by a relative error of at most 0.0003.
Values sent between devices are 32-bit elements; how exact they have to be, the bound alone decides.
No kernel may reach another device: no remote copies, remote signals or barrier semaphores. Data moves between devices by JAX's collectives and lax.ppermute only.
A program may use at most 128 MiB of HBM per device.

v0:
```python
import functools
import math

import jax
import jax.numpy as jnp
import numpy as np
from jax import lax
from jax.experimental import pallas as pl
from jax.experimental.pallas import tpu as pltpu
from jax.sharding import PartitionSpec as P

SWEEPS = 4
QUANTILE = 0.9
PENALTY = 2.0
SMOOTHING = 1.0
HIGHEST = lax.Precision.HIGHEST
HALO = 4
LANES = 128
TILE = 8
UNROLL = 8
PARTS = 8
EDGES_MIB = 52.5
SCALE = 1.0 / 625.0
IN_VMEM = pl.BlockSpec(memory_space=pltpu.VMEM)
IN_HBM = pl.BlockSpec(memory_space=pltpu.HBM)
DMA = pltpu.SemaphoreType.DMA


def f32(*shape):
    return jax.ShapeDtypeStruct(shape, jnp.float32)


def bf16(*shape):
    return jax.ShapeDtypeStruct(shape, jnp.bfloat16)


def call(kernel, outs, in_specs, out_specs, us, scratch=(), mib=20):
    return pl.pallas_call(
        kernel,
        out_shape=outs,
        in_specs=in_specs,
        out_specs=out_specs,
        scratch_shapes=scratch,
        compiler_params=pltpu.CompilerParams(vmem_limit_bytes=int(mib * 2**20)),
        cost_estimate=pl.CostEstimate(flops=int(us * 1e9), bytes_accessed=0, transcendentals=0),
    )


def iota(shape, dim):
    return lax.broadcasted_iota(jnp.int32, shape, dim)


def columns_operator():
    powers = [np.array([1.0])]
    for _ in range(SWEEPS):
        powers.append(np.convolve(powers[-1], [1.0, 0.0, 1.0]))
    weights = [5.0 ** (SWEEPS - 1 - j) for j in range(SWEEPS)] + [1.0]
    inner = np.zeros((LANES, SWEEPS, LANES))
    outer = np.zeros((LANES, SWEEPS, LANES))
    for k in range(SWEEPS):
        band = np.zeros(2 * SWEEPS + 1)
        for j in range(k, SWEEPS + 1):
            reach = j - k
            band[SWEEPS - reach : SWEEPS + reach + 1] += weights[j] * math.comb(j, k) * powers[reach]
        for lane in range(LANES):
            for step in range(-SWEEPS, SWEEPS + 1):
                source = lane + step
                into = inner if 0 <= source < LANES else outer
                into[source % LANES, k, lane] = band[SWEEPS + step]
    inner, outer = (part.reshape(LANES, SWEEPS * LANES) for part in (inner, outer))
    return np.concatenate([inner, inner, outer, outer], axis=0)


def edges_kernel(obs, aux, dual, target, top, bottom, held, sems):
    days, rows, _ = obs.shape
    copies = []
    for day in range(days):
        for k, array in enumerate((obs, aux, dual)):
            copies.append(pltpu.make_async_copy(array.at[day], held.at[day, k], sems.at[day, k]))
    for copy in copies:
        copy.start()
    for day in range(days):
        for k in range(3):
            copies[day * 3 + k].wait()
        target[day] = held[day, 0] - held[day, 1] + held[day, 2]
    low = iota(top.shape, 0) < HALO
    last = rows - TILE
    top[...] = jnp.where(low, target[0, :TILE], pltpu.roll(target[1, :TILE], HALO, 0))
    bottom[...] = jnp.where(low, pltpu.roll(target[1, last:], HALO, 0), target[0, last:])


def split(x):
    high = x.astype(jnp.bfloat16)
    return high, (x - high.astype(jnp.float32)).astype(jnp.bfloat16)


def columns_part(blocks, operator):
    first = iota(blocks[0].shape, 1) < LANES // 2
    stacked = []
    for u in range(1, len(blocks) - 1):
        beside = jnp.where(first, blocks[u + 1], blocks[u - 1])
        stacked.append(jnp.concatenate(split(blocks[u]) + split(beside), axis=1))
    return jnp.dot(jnp.concatenate(stacked, axis=0), operator[...], preferred_element_type=jnp.float32)


def own_kernel(lat_count, target, operator, out):
    blocks, days, rows, _ = out.shape
    lat = lax.axis_index("lat")
    total = rows + TILE
    low = iota((TILE, LANES), 0) < HALO
    inside = jnp.where(low, jnp.where(lat < lat_count - 1, 1.0, 0.0), jnp.where(lat > 0, 1.0, 0.0))
    zero = jnp.zeros((TILE, LANES), jnp.float32)

    def body(group, carry):
        start = group * UNROLL
        held = []
        for u in range(-1, UNROLL + 1):
            j = lax.rem(start + u + blocks, blocks)
            cols = pl.ds(pl.multiple_of(j * LANES, LANES), LANES)
            held.append(jnp.concatenate([target[day, :, cols] for day in range(days)], axis=0))
        parts = columns_part(held, operator)
        for u in range(UNROLL):
            for day in range(days):
                at = (u * days + day) * rows
                now = jnp.concatenate([held[u + 1][day * rows : (day + 1) * rows], zero], axis=0)
                for k in reversed(range(SWEEPS)):
                    upright = pltpu.roll(now, 1, 0) + pltpu.roll(now, total - 1, 0)
                    new = upright[:rows] + parts[at : at + rows, k * LANES : (k + 1) * LANES]
                    if k:
                        now = jnp.concatenate([new, upright[rows:] * inside], axis=0)
                out[start + u, day] = new * SCALE
        return carry

    lax.fori_loop(0, blocks // UNROLL, body, 0)


def halo_kernel(lat_count, own, below, above, operator, after, out):
    blocks, days, rows, _ = own.shape
    row = iota((TILE, LANES), 0)
    low = row < HALO
    begin, end = row == 0, row == TILE - 1
    zero = jnp.zeros((TILE, LANES), jnp.float32)
    lat = lax.axis_index("lat")
    south_scale = jnp.where(lat < lat_count - 1, SCALE, 0.0)
    north_scale = jnp.where(lat > 0, SCALE, 0.0)

    def spread(south, north):
        return (
            (jnp.where(low, pltpu.roll(north, HALO, 0), zero), jnp.where(low, zero, pltpu.roll(south, HALO, 0))),
            (jnp.where(low, north, zero), jnp.where(low, zero, south)),
        )

    def body(group, carry):
        start = group * UNROLL
        held = []
        for u in range(-1, UNROLL + 1):
            j = lax.rem(start + u + blocks, blocks)
            cols = pl.ds(pl.multiple_of(j * LANES, LANES), LANES)
            held.append(jnp.concatenate([below[:, cols], above[:, cols]], axis=0))
        parts = columns_part(held, operator)
        for u in range(UNROLL):
            at = u * 2 * TILE
            now = spread(held[u + 1][:TILE], held[u + 1][TILE:])
            for k in reversed(range(SWEEPS)):
                cols = slice(k * LANES, (k + 1) * LANES)
                part = spread(parts[at : at + TILE, cols], parts[at + TILE : at + 2 * TILE, cols])
                now = tuple(
                    tuple(
                        jnp.where(begin, zero, pltpu.roll(now[day][side], 1, 0))
                        + jnp.where(end, zero, pltpu.roll(now[day][side], TILE - 1, 0))
                        + part[day][side]
                        for side in range(2)
                    )
                    for day in range(days)
                )
            j = start + u
            for day in range(days):
                north = pltpu.roll(now[day][0], HALO, 0) * north_scale
                south = pltpu.roll(now[day][1], HALO, 0) * south_scale
                out[j, day, :TILE] = own[j, day, :TILE] + jnp.where(low, north, zero)
                out[j, day, TILE : rows - TILE] = own[j, day, TILE : rows - TILE]
                out[j, day, rows - TILE :] = own[j, day, rows - TILE :] + jnp.where(low, zero, south)
        return carry

    lax.fori_loop(0, blocks // UNROLL, body, 0)


def stack_left(matrix):
    high, low = split(matrix)
    return jnp.concatenate([high, low, high], axis=1)


def maps_kernel(predictors, inverse_gram, to_coefficients, to_fitted):
    scores = predictors[...]
    contract = (((1,), (1,)), ((), ()))
    direct = lax.dot_general(
        inverse_gram[...], scores, contract, precision=HIGHEST, preferred_element_type=jnp.float32
    )
    back = jnp.dot(scores, direct, precision=HIGHEST, preferred_element_type=jnp.float32)
    to_coefficients[...] = stack_left(direct)
    to_fitted[...] = stack_left(back)


def pairs(smooth, rows, days):
    for r in range(0, rows, 2):
        high, low = split(jnp.concatenate([smooth[pl.ds(r + i, days, stride=rows), :] for i in range(2)], axis=1))
        yield r, jnp.concatenate([high, high, low], axis=0)


def fitted_kernel(smooth, matrix, fitted):
    days = matrix.shape[0]
    rows = smooth.shape[0] // days
    for r, right in pairs(smooth, rows, days):
        both = jnp.dot(matrix[...], right, preferred_element_type=jnp.float32)
        for i in range(2):
            fitted[pl.ds(r + i, days, stride=rows), :] = both[:, i * LANES : (i + 1) * LANES]


def proximal(obs, dual, fitted):
    shifted = obs + dual - fitted
    auxiliary = shifted - jnp.clip(shifted, -(1.0 - QUANTILE) / PENALTY, QUANTILE / PENALTY)
    return auxiliary, shifted - auxiliary


def sums_kernel(obs, aux, dual, fitted, sums):
    blocks, days, rows, _ = fitted.shape

    def body(group, carry):
        primal, change = carry
        for u in range(UNROLL):
            j = group * UNROLL + u
            cols = pl.ds(pl.multiple_of(j * LANES, LANES), LANES)
            for day in range(days):
                dual_now = dual[day, :, cols]
                aux_new, dual_new = proximal(obs[day, :, cols], dual_now, fitted[j, day])
                moved = dual_new - dual_now
                primal += moved * moved
                moved = aux_new - aux[day, :, cols]
                change += moved * moved
        return primal, change

    zero = jnp.zeros((rows, LANES), jnp.float32)
    primal, change = lax.fori_loop(0, blocks // UNROLL, body, (zero, zero))
    primal = jnp.sum(primal, axis=0, keepdims=True)
    change = jnp.sum(change, axis=0, keepdims=True)
    half = LANES // 2
    both = jnp.where(
        iota((1, LANES), 1) < half, primal + pltpu.roll(primal, half, 1), change + pltpu.roll(change, half, 1)
    )
    sums[...] = jnp.broadcast_to(both[None], sums.shape)


def results_kernel(
    smooth, matrix, obs, dual, fitted, after, coefficients, aux_next, dual_next, stacked, held, aux_held, dual_held, sems
):
    depth = matrix.shape[0]
    days_all = matrix.shape[1] // 3
    blocks, days, rows, _ = fitted.shape
    part = depth // PARTS
    copies = []

    def send(source, target, k):
        copies.append(pltpu.make_async_copy(source, target, sems.at[k]))
        copies[-1].start()

    for r, right in pairs(smooth, rows, days_all):
        stacked[r // 2] = right
    for k in range(PARTS):
        for r in range(0, rows, 2):
            both = jnp.dot(
                matrix[k * part : (k + 1) * part, :], stacked[r // 2], preferred_element_type=jnp.float32
            )
            for i in range(2):
                held[pl.ds(k * part * rows + r + i, part, stride=rows), :] = both[:, i * LANES : (i + 1) * LANES]
        span = pl.ds(k * part * rows, part * rows)
        send(held.at[span], coefficients.at[span], k)

    for day in range(days):

        def body(group, carry):
            for u in range(UNROLL):
                j = group * UNROLL + u
                cols = pl.ds(pl.multiple_of(j * LANES, LANES), LANES)
                aux_new, dual_new = proximal(obs[day, :, cols], dual[day, :, cols], fitted[j, day])
                aux_held[day, :, cols] = aux_new
                dual_held[day, :, cols] = dual_new
            return carry

        lax.fori_loop(0, blocks // UNROLL, body, 0)
        send(aux_held.at[day], aux_next.at[day], PARTS + day)
        send(dual_held.at[day], dual_next.at[day], PARTS + days + day)
    for copy in copies:
        copy.wait()


def norms_kernel(sums, primal, change):
    row = jnp.sum(sums[...], axis=0)
    half = iota(row.shape, 1) < LANES // 2
    primal[...] = jnp.sqrt(jnp.sum(jnp.where(half, row, 0.0), axis=1, keepdims=True))
    change[...] = PENALTY * jnp.sqrt(jnp.sum(jnp.where(half, 0.0, row), axis=1, keepdims=True))


def local(lat_count, lon_count, observations, aux_state, dual_state, predictors, inverse_gram):
    days, rows, columns = observations.shape
    blocks = columns // LANES
    all_days = days * lon_count
    depth = inverse_gram.shape[0]
    field = f32(blocks, days, rows, LANES)
    state = (observations, aux_state, dual_state)
    slab = f32(days, rows, columns)
    tile = f32(TILE, columns)
    target, top, bottom = call(
        edges_kernel,
        (slab, tile, tile),
        [IN_HBM] * 3,
        (IN_VMEM,) * 3,
        2.0,
        [pltpu.VMEM((days, 3, rows, columns), jnp.float32), DMA((days, 3))],
        EDGES_MIB,
    )(*state)
    below = lax.ppermute(top, "lat", [((i + 1) % lat_count, i) for i in range(lat_count)])
    above = lax.ppermute(bottom, "lat", [(i, (i + 1) % lat_count) for i in range(lat_count)])
    operator = jnp.asarray(columns_operator(), jnp.bfloat16)
    own = call(functools.partial(own_kernel, lat_count), field, [IN_VMEM] * 2, IN_VMEM, 3.0)(target, operator)
    to_coefficients, to_fitted = call(
        maps_kernel,
        (bf16(depth, 3 * all_days), bf16(all_days, 3 * all_days)),
        [IN_VMEM] * 2,
        (IN_VMEM, IN_VMEM),
        2.0,
    )(predictors, inverse_gram)
    smooth = call(functools.partial(halo_kernel, lat_count), field, [IN_VMEM] * 5, IN_VMEM, 1.5)(
        own, below, above, operator, to_fitted
    )
    smooth = lax.all_to_all(smooth, "lon", 0, 0, tiled=True).reshape(all_days * rows, LANES)
    fitted = call(fitted_kernel, f32(all_days * rows, LANES), [IN_VMEM] * 2, IN_VMEM, 2.0)(smooth, to_fitted)
    fitted = lax.all_to_all(fitted.reshape(field.shape), "lon", 0, 0, tiled=True)
    devices = lat_count * lon_count
    sums = call(sums_kernel, f32(devices, 1, LANES), [IN_VMEM] * 4, IN_VMEM, 1.0)(
        *state, fitted
    )
    coefficients, aux_next, dual_next = call(
        results_kernel,
        (f32(depth * rows, LANES), slab, slab),
        [IN_VMEM] * 5 + [IN_HBM],
        (IN_HBM,) * 3,
        5.0,
        [
            pltpu.VMEM((rows // 2, 3 * all_days, 2 * LANES), jnp.bfloat16),
            pltpu.VMEM((depth * rows, LANES), jnp.float32),
            pltpu.VMEM(slab.shape, jnp.float32),
            pltpu.VMEM(slab.shape, jnp.float32),
            DMA((PARTS + 2 * days,)),
        ],
    )(smooth, to_coefficients, observations, dual_state, fitted, sums)
    coefficients = coefficients.reshape(depth, rows, LANES)
    sums = lax.all_to_all(sums, ("lat", "lon"), 0, 0, tiled=True)
    primal, change = call(norms_kernel, (f32(1, 1), f32(1, 1)), [IN_VMEM], (IN_VMEM, IN_VMEM), 0.5)(sums)
    return (coefficients, aux_next, dual_next, primal.reshape(()), change.reshape(()))


def solution(mesh):
    in_specs = (P("lon", "lat", None), P("lon", "lat", None), P("lon", "lat", None), P(), P())
    out_specs = (P(None, "lat", "lon"), P("lon", "lat", None), P("lon", "lat", None), P(), P())
    body = functools.partial(local, mesh.shape["lat"], mesh.shape["lon"])
    return jax.shard_map(body, mesh=mesh, in_specs=in_specs, out_specs=out_specs, check_vma=False)
```

profile of v0, /device:TPU:1, one launch (start us, length us, event | category | flops | bytes accessed | tf_op | source)
XLA Modules:
  0.0 70.7 jit_solution(13202558344001775349)
XLA Ops:
  0.6 0.0 copy-start.5
  0.6 1.8 %shard_map.101 = (f32[2,24,4096]{2,1,0:T(8,128)S(1)}, f32[8,4096]{1,0:T(8,128)S(1)}, f32[8,4096]{1,0:T(8,128)S(1)}) custom-call(f32[2,24,4096]{2,1,0:T(8,128)} %obs.5, f32[2,24,4096]{2,1,0:T(8,128)} %aux.3, f32[2,24,4096]{2,1,0:T(8,128)} %dual.5), custom_call_target="tpu_custom_call" | custom-call | flops 2000000000 | tf_op jit(solution)/shard_map/pallas_call | solution.py:312
  2.4 0.0 copy-start
  2.5 0.0 copy-start.4
  2.5 4.7 %collective-permute-start = (f32[8,4096]{1,0:T(8,128)S(1)}, f32[8,4096]{1,0:T(8,128)S(1)}, u32[]{:S(2)}, u32[]{:S(2)}) collective-permute-start(f32[8,4096]{1,0:T(8,128)S(1)} %get-tuple-element.16), channel_id=1, source_target_pairs={{32,0},{64,32},{96,64},{0,96},{33,1},{65,33},{97,65},{1,97},{34,2}... | collective-permute-start | bytes 393224 | tf_op jit(solution)/shard_map/ppermute | solution.py:321
  7.1 0.0 collective-permute-start.1
  7.1 0.0 copy-done.5
  7.1 1.9 %shard_map.102.own = f32[32,2,24,128]{3,2,1,0:T(8,128)S(1)} custom-call(f32[2,24,4096]{2,1,0:T(8,128)S(1)} %get-tuple-element.15.target, bf16[512,512]{1,0:T(8,128)(2,1)S(1)} %copy-done.5), custom_call_target="tpu_custom_call" | custom-call | flops 3000000000 | tf_op jit(solution)/shard_map/pallas_call | solution.py:324
  9.0 0.0 copy-done
  9.0 0.0 copy-done.4
  9.0 1.4 %shard_map.103 = (bf16[512,192]{1,0:T(8,128)(2,1)S(1)}, bf16[64,192]{1,0:T(8,128)(2,1)S(1)}) custom-call(f32[64,512]{1,0:T(8,128)S(1)} %copy-done.4, f32[512,512]{1,0:T(8,128)S(1)} %copy-done), custom_call_target="tpu_custom_call" | custom-call | flops 2000000000 | tf_op jit(solution)/shard_map/pallas_call | solution.py:325
  10.4 0.0 collective-permute-done.below
  10.4 1.7 %collective-permute-done.1.above = f32[8,4096]{1,0:T(8,128)S(1)} collective-permute-done((f32[8,4096]{1,0:T(8,128)S(1)}, f32[8,4096]{1,0:T(8,128)S(1)}, u32[]{:S(2)}, u32[]{:S(2)}) %collective-permute-start.1) | collective-permute-done | bytes 131104 | tf_op jit(solution)/shard_map/ppermute | solution.py:322
  12.2 1.4 %shard_map.104 = f32[32,2,24,128]{3,2,1,0:T(8,128)S(1)} custom-call(f32[32,2,24,128]{3,2,1,0:T(8,128)S(1)} %shard_map.102.own, f32[8,4096]{1,0:T(8,128)S(1)} %collective-permute-done.below, f32[8,4096]{1,0:T(8,128)S(1)} %collective-permute-done.1.above, bf16[512,512]{1,0:T(8,128)(2,1)S(1)} %copy-done.5, bf16[64,192]{1,0:T(8,128)(2,1)S(1)} %get-tuple-element.18.after.matrix), custom_call_target="tpu_custom_call" | custom-call | flops 1500000000 | tf_op jit(solution)/shard_map/pallas_call | solution.py:332
  13.6 0.0 copy-start.1
  13.6 0.0 copy-start.2
  13.6 0.0 copy-start.3
  13.6 23.3 %all_to_all.15 = f32[32,2,24,128]{3,2,1,0:T(8,128)S(1)} all-to-all(f32[32,2,24,128]{3,2,1,0:T(8,128)S(1)} %shard_map.104), channel_id=1, replica_groups=mesh['lat'=4,'lon'=32] {'lon'}, dimensions={0} | all-to-all | bytes 1572864 | tf_op jit(solution)/shard_map/all_to_all | solution.py:335
  37.0 0.4 shard_map.105
  37.3 17.9 %all_to_all.16.fitted = f32[32,2,24,128]{3,2,1,0:T(8,128)S(1)} all-to-all(f32[32,2,24,128]{3,2,1,0:T(8,128)S(1)} %bitcast.7), channel_id=1, replica_groups=mesh['lat'=4,'lon'=32] {'lon'}, dimensions={0} | all-to-all | bytes 1572864 | tf_op jit(solution)/shard_map/all_to_all | solution.py:337
  55.2 0.0 copy-done.1
  55.2 0.0 copy-done.2
  55.2 0.0 copy-done.3
  55.2 1.1 %shard_map.106.after = f32[128,1,128]{2,1,0:T(1,128)} custom-call(f32[2,24,4096]{2,1,0:T(8,128)S(1)} %copy-done.2, f32[2,24,4096]{2,1,0:T(8,128)S(1)} %copy-done.1, f32[2,24,4096]{2,1,0:T(8,128)S(1)} %copy-done.3, f32[32,2,24,128]{3,2,1,0:T(8,128)S(1)} %all_to_all.16.fitted), custom_call_target="tpu_custom_call" | custom-call | flops 1000000000 | tf_op jit(solution)/shard_map/pallas_call | solution.py:339
  56.3 3.9 %all-to-all-start.2 = ((f32[128,1,128]{2,1,0:T(1,128)}), f32[128,1,128]{2,1,0:T(1,128)S(1)}, u32[]{:S(2)}, u32[]{:S(2)}) async-start(f32[128,1,128]{2,1,0:T(1,128)} %shard_map.106.after), calls=%async_computation.2 | async-start | bytes 131072 | tf_op jit(solution)/shard_map/all_to_all | solution.py:357
  60.2 3.7 %shard_map.107 = (f32[12288,128]{1,0:T(8,128)}, f32[2,24,4096]{2,1,0:T(8,128)}, f32[2,24,4096]{2,1,0:T(8,128)}) custom-call(f32[1536,128]{1,0:T(8,128)S(1)} %bitcast.6, bf16[512,192]{1,0:T(8,128)(2,1)S(1)} %get-tuple-element.19.matrix, f32[2,24,4096]{2,1,0:T(8,128)S(1)} %copy-done.2, f32[2,24,4096]{2,1,0:T(8,128)S(1)} %copy-done.3, ...), custom_call_target="tpu_custom_call" | custom-call | flops 5000000000 | tf_op jit(solution)/shard_map/pallas_call | solution.py:342
  63.9 6.1 %all-to-all-done.2.sums = f32[128,1,128]{2,1,0:T(1,128)S(1)} async-done(((f32[128,1,128]{2,1,0:T(1,128)}), f32[128,1,128]{2,1,0:T(1,128)S(1)}, u32[]{:S(2)}, u32[]{:S(2)}) %all-to-all-start.2) | async-done | bytes 65568 | tf_op jit(solution)/shard_map/all_to_all | solution.py:357
  70.0 0.7 %shard_map.108 = (f32[1,1]{1,0:T(1,128)}, f32[1,1]{1,0:T(1,128)}) custom-call(f32[128,1,128]{2,1,0:T(1,128)S(1)} %all-to-all-done.2.sums), custom_call_target="tpu_custom_call" | custom-call | flops 500000000 | tf_op jit(solution)/shard_map/pallas_call | solution.py:358
Async XLA Ops:
  0.6 6.5 %copy-start.5 = (bf16[512,512]{1,0:T(8,128)(2,1)S(1)}, bf16[512,512]{1,0:T(8,128)(2,1)}, u32[]{:S(2)}) copy-start(bf16[512,512]{1,0:T(8,128)(2,1)} %constant.2.clone.operator) | copy-start | bytes 1572868
  2.4 6.6 %copy-start = (f32[512,512]{1,0:T(8,128)S(1)}, f32[512,512]{1,0:T(8,128)}, u32[]{:S(2)}) copy-start(f32[512,512]{1,0:T(8,128)} %inverse_gram.1) | copy-start | bytes 3145732
  2.5 6.6 %copy-start.4 = (f32[64,512]{1,0:T(8,128)S(1)}, f32[64,512]{1,0:T(8,128)}, u32[]{:S(2)}) copy-start(f32[64,512]{1,0:T(8,128)} %predictors.1) | copy-start | bytes 393220
  2.5 8.0 %collective-permute-start = (f32[8,4096]{1,0:T(8,128)S(1)}, f32[8,4096]{1,0:T(8,128)S(1)}, u32[]{:S(2)}, u32[]{:S(2)}) collective-permute-start(f32[8,4096]{1,0:T(8,128)S(1)} %get-tuple-element.16), channel_id=1, source_target_pairs={{32,0},{64,32},{96,64},{0,96},{33,1},{65,33},{97,65},{1,97},{34,2}... | collective-permute-start | bytes 393224 | tf_op jit(solution)/shard_map/ppermute | solution.py:321
  7.1 5.0 %collective-permute-start.1 = (f32[8,4096]{1,0:T(8,128)S(1)}, f32[8,4096]{1,0:T(8,128)S(1)}, u32[]{:S(2)}, u32[]{:S(2)}) collective-permute-start(f32[8,4096]{1,0:T(8,128)S(1)} %get-tuple-element.17), channel_id=1, source_target_pairs={{0,32},{32,64},{64,96},{96,0},{1,33},{33,65},{65,97},{97,1},{2,34}... | collective-permute-start | bytes 393224 | tf_op jit(solution)/shard_map/ppermute | solution.py:322
  13.6 41.6 %copy-start.1 = (f32[2,24,4096]{2,1,0:T(8,128)S(1)}, f32[2,24,4096]{2,1,0:T(8,128)}, u32[]{:S(2)}) copy-start(f32[2,24,4096]{2,1,0:T(8,128)} %aux.3) | copy-start | bytes 2359300
  13.6 41.6 %copy-start.2 = (f32[2,24,4096]{2,1,0:T(8,128)S(1)}, f32[2,24,4096]{2,1,0:T(8,128)}, u32[]{:S(2)}) copy-start(f32[2,24,4096]{2,1,0:T(8,128)} %obs.5) | copy-start | bytes 2359300
  13.6 41.6 %copy-start.3 = (f32[2,24,4096]{2,1,0:T(8,128)S(1)}, f32[2,24,4096]{2,1,0:T(8,128)}, u32[]{:S(2)}) copy-start(f32[2,24,4096]{2,1,0:T(8,128)} %dual.5) | copy-start | bytes 2359300
  56.3 13.6 %all-to-all-start.2 = ((f32[128,1,128]{2,1,0:T(1,128)}), f32[128,1,128]{2,1,0:T(1,128)S(1)}, u32[]{:S(2)}, u32[]{:S(2)}) async-start(f32[128,1,128]{2,1,0:T(1,128)} %shard_map.106.after), calls=%async_computation.2 | async-start | bytes 131072 | tf_op jit(solution)/shard_map/all_to_all | solution.py:357
where the time goes:
time: 71 us; the launch traced here: 70.7 us
  blocking collectives  41.2 us (58%)
  Pallas kernels  12.3 us (17%)
  starting transfers between devices  8.56 us (12%)
  waiting for transfers between devices  7.82 us (11%)
  between operations  0.75 us (1%)
    all_to_all x1, blocking collectives, local(): lax.all_to_all(smooth, 'lon', 0, 0, tiled=True)  23.3 us
    all_to_all x1, blocking collectives, local(): lax.all_to_all(fitted.reshape(field.shape), 'lon', 0, 0, tiled=True)  17.9 us
    all_to_all x1, waiting for transfers between devices, local(): sums = lax.all_to_all(sums, ('lat', 'lon'), 0, 0, tiled=True)  6.08 us
    ppermute x1, starting transfers between devices, local(): lax.ppermute(top, 'lat', [((i + 1) % lat_count, i) for i in range(lat_cou...  4.66 us
    all_to_all x1, starting transfers between devices, local(): sums = lax.all_to_all(sums, ('lat', 'lon'), 0, 0, tiled=True)  3.9 us
    pallas_call x1, Pallas kernels, local(): call(results_kernel, (f32(depth * rows, LANES), slab, slab), [IN_VMEM] *...  3.65 us
    pallas_call x1, Pallas kernels, local(): call(functools.partial(own_kernel, lat_count), field, [IN_VMEM] * 2, IN_V...  1.86 us
    pallas_call x1, Pallas kernels, local(): call(edges_kernel, (slab, tile, tile), [IN_HBM] * 3, (IN_VMEM,) * 3, 2.0,...  1.8 us
  transfers between devices with their start and end apart: 3, of which 2 were waited for; matrix products, arithmetic and copies ran while one was open for 0% of the time, Pallas kernels for 10%

commit v1 on v0

--- a/solution.py
+++ b/solution.py
@@ -18,6 +18,8 @@
 LANES = 128
 TILE = 8
 UNROLL = 8
+OWN_UNROLL = 32
+HALO_UNROLL = 32
 PARTS = 8
 EDGES_MIB = 52.5
 SCALE = 1.0 / 625.0
@@ -71,7 +73,7 @@
     return np.concatenate([inner, inner, outer, outer], axis=0)
 
 
-def edges_kernel(obs, aux, dual, target, top, bottom, held, sems):
+def edges_kernel(obs, aux, dual, target, bottom, top, held, sems):
     days, rows, _ = obs.shape
     copies = []
     for day in range(days):
@@ -112,14 +114,14 @@
     zero = jnp.zeros((TILE, LANES), jnp.float32)
 
     def body(group, carry):
-        start = group * UNROLL
+        start = group * OWN_UNROLL
         held = []
-        for u in range(-1, UNROLL + 1):
+        for u in range(-1, OWN_UNROLL + 1):
             j = lax.rem(start + u + blocks, blocks)
             cols = pl.ds(pl.multiple_of(j * LANES, LANES), LANES)
             held.append(jnp.concatenate([target[day, :, cols] for day in range(days)], axis=0))
         parts = columns_part(held, operator)
-        for u in range(UNROLL):
+        for u in range(OWN_UNROLL):
             for day in range(days):
                 at = (u * days + day) * rows
                 now = jnp.concatenate([held[u + 1][day * rows : (day + 1) * rows], zero], axis=0)
@@ -131,10 +133,10 @@
                 out[start + u, day] = new * SCALE
         return carry
 
-    lax.fori_loop(0, blocks // UNROLL, body, 0)
-
-
-def halo_kernel(lat_count, own, below, above, operator, after, out):
+    lax.fori_loop(0, blocks // OWN_UNROLL, body, 0)
+
+
+def halo_kernel(lat_count, own, above, below, operator, after, out):
     blocks, days, rows, _ = own.shape
     row = iota((TILE, LANES), 0)
     low = row < HALO
@@ -151,14 +153,14 @@
         )
 
     def body(group, carry):
-        start = group * UNROLL
+        start = group * HALO_UNROLL
         held = []
-        for u in range(-1, UNROLL + 1):
+        for u in range(-1, HALO_UNROLL + 1):
             j = lax.rem(start + u + blocks, blocks)
             cols = pl.ds(pl.multiple_of(j * LANES, LANES), LANES)
             held.append(jnp.concatenate([below[:, cols], above[:, cols]], axis=0))
         parts = columns_part(held, operator)
-        for u in range(UNROLL):
+        for u in range(HALO_UNROLL):
             at = u * 2 * TILE
             now = spread(held[u + 1][:TILE], held[u + 1][TILE:])
             for k in reversed(range(SWEEPS)):
@@ -182,7 +184,7 @@
                 out[j, day, rows - TILE :] = own[j, day, rows - TILE :] + jnp.where(low, zero, south)
         return carry
 
-    lax.fori_loop(0, blocks // UNROLL, body, 0)
+    lax.fori_loop(0, blocks // HALO_UNROLL, body, 0)
 
 
 def stack_left(matrix):
@@ -190,13 +192,15 @@
     return jnp.concatenate([high, low, high], axis=1)
 
 
+def stack_right(matrix):
+    high, low = split(matrix)
+    return jnp.concatenate([high, high, low], axis=0)
+
+
 def maps_kernel(predictors, inverse_gram, to_coefficients, to_fitted):
     scores = predictors[...]
-    contract = (((1,), (1,)), ((), ()))
-    direct = lax.dot_general(
-        inverse_gram[...], scores, contract, precision=HIGHEST, preferred_element_type=jnp.float32
-    )
-    back = jnp.dot(scores, direct, precision=HIGHEST, preferred_element_type=jnp.float32)
+    direct = jnp.dot(stack_left(inverse_gram[...]), stack_right(scores.T), preferred_element_type=jnp.float32)
+    back = jnp.dot(stack_left(scores), stack_right(direct), preferred_element_type=jnp.float32)
     to_coefficients[...] = stack_left(direct)
     to_fitted[...] = stack_left(back)
 
@@ -261,7 +265,7 @@
 
     def send(source, target, k):
         copies.append(pltpu.make_async_copy(source, target, sems.at[k]))
-        copies[-1].start()
+        copies[-1].start(priority=k % 2)
 
     for r, right in pairs(smooth, rows, days_all):
         stacked[r // 2] = right
@@ -309,7 +313,7 @@
     state = (observations, aux_state, dual_state)
     slab = f32(days, rows, columns)
     tile = f32(TILE, columns)
-    target, top, bottom = call(
+    target, bottom, top = call(
         edges_kernel,
         (slab, tile, tile),
         [IN_HBM] * 3,
@@ -318,8 +322,8 @@
         [pltpu.VMEM((days, 3, rows, columns), jnp.float32), DMA((days, 3))],
         EDGES_MIB,
     )(*state)
+    above = lax.ppermute(bottom, "lat", [(i, (i + 1) % lat_count) for i in range(lat_count)])
     below = lax.ppermute(top, "lat", [((i + 1) % lat_count, i) for i in range(lat_count)])
-    above = lax.ppermute(bottom, "lat", [(i, (i + 1) % lat_count) for i in range(lat_count)])
     operator = jnp.asarray(columns_operator(), jnp.bfloat16)
     own = call(functools.partial(own_kernel, lat_count), field, [IN_VMEM] * 2, IN_VMEM, 3.0)(target, operator)
     to_coefficients, to_fitted = call(
@@ -330,7 +334,7 @@
         2.0,
     )(predictors, inverse_gram)
     smooth = call(functools.partial(halo_kernel, lat_count), field, [IN_VMEM] * 5, IN_VMEM, 1.5)(
-        own, below, above, operator, to_fitted
+        own, above, below, operator, to_fitted
     )
     smooth = lax.all_to_all(smooth, "lon", 0, 0, tiled=True).reshape(all_days * rows, LANES)
     fitted = call(fitted_kernel, f32(all_days * rows, LANES), [IN_VMEM] * 2, IN_VMEM, 2.0)(smooth, to_fitted)

time: 71 us -> 69.5 us (0.979)
  starting transfers between devices: 8.56 us -> 10.5 us
  waiting for transfers between devices: 7.82 us -> 6.54 us
  Pallas kernels: 12.3 us -> 11.1 us
  blocking collectives: 41.2 us -> 40.4 us
    ppermute x1, starting transfers between devices: 0.01 us -> 2.54 us  [local(): lax.ppermute(bottom, 'lat', [(i, (i + 1) % lat_count) for i in range(lat_...]
    ppermute x1, starting transfers between devices: 4.66 us -> 2.2 us  [local(): lax.ppermute(top, 'lat', [((i + 1) % lat_count, i) for i in range(lat_cou...]
    all_to_all x1, starting transfers between devices: 3.9 us -> 5.76 us  [local(): sums = lax.all_to_all(sums, ('lat', 'lon'), 0, 0, tiled=True)]
    ppermute x1, waiting for transfers between devices: 1.73 us -> 0.58 us  [local(): lax.ppermute(bottom, 'lat', [(i, (i + 1) % lat_count) for i in range(lat_...]
    all_to_all x1, blocking collectives: 23.3 us -> 22.5 us  [local(): lax.all_to_all(smooth, 'lon', 0, 0, tiled=True)]
  transfers between devices with their start and end apart: 3 -> 3, of which waited for: 2 -> 2; matrix products, arithmetic and copies ran while one was open for 0% -> 0% of each run, Pallas kernels for 10% -> 9%
where the time goes in v1:
time: 69.5 us; the launch traced here: 69.2 us
  blocking collectives  40.4 us (58%)
  Pallas kernels  11.1 us (16%)
  starting transfers between devices  10.5 us (15%)
  waiting for transfers between devices  6.54 us (9%)
  between operations  0.75 us (1%)
    all_to_all x1, blocking collectives, local(): lax.all_to_all(smooth, 'lon', 0, 0, tiled=True)  22.5 us
    all_to_all x1, blocking collectives, local(): lax.all_to_all(fitted.reshape(field.shape), 'lon', 0, 0, tiled=True)  17.9 us
    all_to_all x1, waiting for transfers between devices, local(): sums = lax.all_to_all(sums, ('lat', 'lon'), 0, 0, tiled=True)  5.95 us
    all_to_all x1, starting transfers between devices, local(): sums = lax.all_to_all(sums, ('lat', 'lon'), 0, 0, tiled=True)  5.76 us
    pallas_call x1, Pallas kernels, local(): call(results_kernel, (f32(depth * rows, LANES), slab, slab), [IN_VMEM] *...  3.65 us
    ppermute x1, starting transfers between devices, local(): lax.ppermute(bottom, 'lat', [(i, (i + 1) % lat_count) for i in range(lat_...  2.54 us
    ppermute x1, starting transfers between devices, local(): lax.ppermute(top, 'lat', [((i + 1) % lat_count, i) for i in range(lat_cou...  2.2 us
    pallas_call x1, Pallas kernels, local(): call(edges_kernel, (slab, tile, tile), [IN_HBM] * 3, (IN_VMEM,) * 3, 2.0,...  1.8 us
  transfers between devices with their start and end apart: 3, of which 2 were waited for; matrix products, arithmetic and copies ran while one was open for 0% of the time, Pallas kernels for 9%

profile of v1, /device:TPU:1, one launch (start us, length us, event | category | flops | bytes accessed | tf_op | source)
XLA Modules:
  0.0 69.2 jit_solution(8259774581621217265)
XLA Ops:
  0.6 0.0 copy-start.5
  0.6 1.8 %shard_map.101 = (f32[2,24,4096]{2,1,0:T(8,128)S(1)}, f32[8,4096]{1,0:T(8,128)S(1)}, f32[8,4096]{1,0:T(8,128)S(1)}) custom-call(f32[2,24,4096]{2,1,0:T(8,128)} %obs.5, f32[2,24,4096]{2,1,0:T(8,128)} %aux.3, f32[2,24,4096]{2,1,0:T(8,128)} %dual.5), custom_call_target="tpu_custom_call" | custom-call | flops 2000000000 | tf_op jit(solution)/shard_map/pallas_call | solution.py:316
  2.4 0.0 copy-start
  2.5 0.0 copy-start.4
  2.5 2.5 %collective-permute-start = (f32[8,4096]{1,0:T(8,128)S(1)}, f32[8,4096]{1,0:T(8,128)S(1)}, u32[]{:S(2)}, u32[]{:S(2)}) collective-permute-start(f32[8,4096]{1,0:T(8,128)S(1)} %get-tuple-element.16), channel_id=1, source_target_pairs={{0,32},{32,64},{64,96},{96,0},{1,33},{33,65},{65,97},{97,1},{2,34}... | collective-permute-start | bytes 393224 | tf_op jit(solution)/shard_map/ppermute | solution.py:325
  5.0 2.2 %collective-permute-start.1 = (f32[8,4096]{1,0:T(8,128)S(1)}, f32[8,4096]{1,0:T(8,128)S(1)}, u32[]{:S(2)}, u32[]{:S(2)}) collective-permute-start(f32[8,4096]{1,0:T(8,128)S(1)} %get-tuple-element.17), channel_id=1, source_target_pairs={{32,0},{64,32},{96,64},{0,96},{33,1},{65,33},{97,65},{1,97},{34,2}... | collective-permute-start | bytes 393224 | tf_op jit(solution)/shard_map/ppermute | solution.py:326
  7.2 0.0 copy-done.5
  7.2 1.5 %shard_map.102.own = f32[32,2,24,128]{3,2,1,0:T(8,128)S(1)} custom-call(f32[2,24,4096]{2,1,0:T(8,128)S(1)} %get-tuple-element.15.target, bf16[512,512]{1,0:T(8,128)(2,1)S(1)} %copy-done.5), custom_call_target="tpu_custom_call" | custom-call | flops 3000000000 | tf_op jit(solution)/shard_map/pallas_call | solution.py:328
  8.7 0.0 copy-done
  8.8 0.0 copy-done.4
  8.8 1.0 %shard_map.103 = (bf16[512,192]{1,0:T(8,128)(2,1)S(1)}, bf16[64,192]{1,0:T(8,128)(2,1)S(1)}) custom-call(f32[64,512]{1,0:T(8,128)S(1)} %copy-done.4, f32[512,512]{1,0:T(8,128)S(1)} %copy-done), custom_call_target="tpu_custom_call" | custom-call | flops 2000000000 | tf_op jit(solution)/shard_map/pallas_call | solution.py:329
  9.8 0.6 collective-permute-done.above
  10.4 0.0 collective-permute-done.1.below
  10.4 0.9 %shard_map.104 = f32[32,2,24,128]{3,2,1,0:T(8,128)S(1)} custom-call(f32[32,2,24,128]{3,2,1,0:T(8,128)S(1)} %shard_map.102.own, f32[8,4096]{1,0:T(8,128)S(1)} %collective-permute-done.above, f32[8,4096]{1,0:T(8,128)S(1)} %collective-permute-done.1.below, bf16[512,512]{1,0:T(8,128)(2,1)S(1)} %copy-done.5, bf16[64,192]{1,0:T(8,128)(2,1)S(1)} %get-tuple-element.18.after.matrix), custom_call_target="tpu_custom_call" | custom-call | flops 1500000000 | tf_op jit(solution)/shard_map/pallas_call | solution.py:336
  11.3 0.0 copy-start.1
  11.3 0.0 copy-start.2
  11.3 0.0 copy-start.3
  11.3 22.5 %all_to_all.15 = f32[32,2,24,128]{3,2,1,0:T(8,128)S(1)} all-to-all(f32[32,2,24,128]{3,2,1,0:T(8,128)S(1)} %shard_map.104), channel_id=1, replica_groups=mesh['lat'=4,'lon'=32] {'lon'}, dimensions={0} | all-to-all | bytes 1572864 | tf_op jit(solution)/shard_map/all_to_all | solution.py:339
  33.8 0.4 shard_map.105
  34.1 17.9 %all_to_all.16.fitted = f32[32,2,24,128]{3,2,1,0:T(8,128)S(1)} all-to-all(f32[32,2,24,128]{3,2,1,0:T(8,128)S(1)} %bitcast.7), channel_id=1, replica_groups=mesh['lat'=4,'lon'=32] {'lon'}, dimensions={0} | all-to-all | bytes 1572864 | tf_op jit(solution)/shard_map/all_to_all | solution.py:341
  52.0 0.0 copy-done.1
  52.0 0.0 copy-done.2
  52.0 0.0 copy-done.3
  52.0 1.1 %shard_map.106.after = f32[128,1,128]{2,1,0:T(1,128)} custom-call(f32[2,24,4096]{2,1,0:T(8,128)S(1)} %copy-done.2, f32[2,24,4096]{2,1,0:T(8,128)S(1)} %copy-done.1, f32[2,24,4096]{2,1,0:T(8,128)S(1)} %copy-done.3, f32[32,2,24,128]{3,2,1,0:T(8,128)S(1)} %all_to_all.16.fitted), custom_call_target="tpu_custom_call" | custom-call | flops 1000000000 | tf_op jit(solution)/shard_map/pallas_call | solution.py:343
  53.1 5.8 %all-to-all-start.2 = ((f32[128,1,128]{2,1,0:T(1,128)}), f32[128,1,128]{2,1,0:T(1,128)S(1)}, u32[]{:S(2)}, u32[]{:S(2)}) async-start(f32[128,1,128]{2,1,0:T(1,128)} %shard_map.106.after), calls=%async_computation.2 | async-start | bytes 131072 | tf_op jit(solution)/shard_map/all_to_all | solution.py:361
  58.9 3.6 %shard_map.107 = (f32[12288,128]{1,0:T(8,128)}, f32[2,24,4096]{2,1,0:T(8,128)}, f32[2,24,4096]{2,1,0:T(8,128)}) custom-call(f32[1536,128]{1,0:T(8,128)S(1)} %bitcast.6, bf16[512,192]{1,0:T(8,128)(2,1)S(1)} %get-tuple-element.19.matrix, f32[2,24,4096]{2,1,0:T(8,128)S(1)} %copy-done.2, f32[2,24,4096]{2,1,0:T(8,128)S(1)} %copy-done.3, ...), custom_call_target="tpu_custom_call" | custom-call | flops 5000000000 | tf_op jit(solution)/shard_map/pallas_call | solution.py:346
  62.6 5.9 %all-to-all-done.2.sums = f32[128,1,128]{2,1,0:T(1,128)S(1)} async-done(((f32[128,1,128]{2,1,0:T(1,128)}), f32[128,1,128]{2,1,0:T(1,128)S(1)}, u32[]{:S(2)}, u32[]{:S(2)}) %all-to-all-start.2) | async-done | bytes 65568 | tf_op jit(solution)/shard_map/all_to_all | solution.py:361
  68.5 0.7 %shard_map.108 = (f32[1,1]{1,0:T(1,128)}, f32[1,1]{1,0:T(1,128)}) custom-call(f32[128,1,128]{2,1,0:T(1,128)S(1)} %all-to-all-done.2.sums), custom_call_target="tpu_custom_call" | custom-call | flops 500000000 | tf_op jit(solution)/shard_map/pallas_call | solution.py:362
Async XLA Ops:
  0.6 6.6 %copy-start.5 = (bf16[512,512]{1,0:T(8,128)(2,1)S(1)}, bf16[512,512]{1,0:T(8,128)(2,1)}, u32[]{:S(2)}) copy-start(bf16[512,512]{1,0:T(8,128)(2,1)} %constant.2.clone.operator) | copy-start | bytes 1572868
  2.4 6.3 %copy-start = (f32[512,512]{1,0:T(8,128)S(1)}, f32[512,512]{1,0:T(8,128)}, u32[]{:S(2)}) copy-start(f32[512,512]{1,0:T(8,128)} %inverse_gram.1) | copy-start | bytes 3145732
  2.5 6.3 %copy-start.4 = (f32[64,512]{1,0:T(8,128)S(1)}, f32[64,512]{1,0:T(8,128)}, u32[]{:S(2)}) copy-start(f32[64,512]{1,0:T(8,128)} %predictors.1) | copy-start | bytes 393220
  2.5 7.9 %collective-permute-start = (f32[8,4096]{1,0:T(8,128)S(1)}, f32[8,4096]{1,0:T(8,128)S(1)}, u32[]{:S(2)}, u32[]{:S(2)}) collective-permute-start(f32[8,4096]{1,0:T(8,128)S(1)} %get-tuple-element.16), channel_id=1, source_target_pairs={{0,32},{32,64},{64,96},{96,0},{1,33},{33,65},{65,97},{97,1},{2,34}... | collective-permute-start | bytes 393224 | tf_op jit(solution)/shard_map/ppermute | solution.py:325
  5.0 5.3 %collective-permute-start.1 = (f32[8,4096]{1,0:T(8,128)S(1)}, f32[8,4096]{1,0:T(8,128)S(1)}, u32[]{:S(2)}, u32[]{:S(2)}) collective-permute-start(f32[8,4096]{1,0:T(8,128)S(1)} %get-tuple-element.17), channel_id=1, source_target_pairs={{32,0},{64,32},{96,64},{0,96},{33,1},{65,33},{97,65},{1,97},{34,2}... | collective-permute-start | bytes 393224 | tf_op jit(solution)/shard_map/ppermute | solution.py:326
  11.3 40.8 %copy-start.1 = (f32[2,24,4096]{2,1,0:T(8,128)S(1)}, f32[2,24,4096]{2,1,0:T(8,128)}, u32[]{:S(2)}) copy-start(f32[2,24,4096]{2,1,0:T(8,128)} %aux.3) | copy-start | bytes 2359300
  11.3 40.7 %copy-start.2 = (f32[2,24,4096]{2,1,0:T(8,128)S(1)}, f32[2,24,4096]{2,1,0:T(8,128)}, u32[]{:S(2)}) copy-start(f32[2,24,4096]{2,1,0:T(8,128)} %obs.5) | copy-start | bytes 2359300
  11.3 40.7 %copy-start.3 = (f32[2,24,4096]{2,1,0:T(8,128)S(1)}, f32[2,24,4096]{2,1,0:T(8,128)}, u32[]{:S(2)}) copy-start(f32[2,24,4096]{2,1,0:T(8,128)} %dual.5) | copy-start | bytes 2359300
  53.1 15.4 %all-to-all-start.2 = ((f32[128,1,128]{2,1,0:T(1,128)}), f32[128,1,128]{2,1,0:T(1,128)S(1)}, u32[]{:S(2)}, u32[]{:S(2)}) async-start(f32[128,1,128]{2,1,0:T(1,128)} %shard_map.106.after), calls=%async_computation.2 | async-start | bytes 131072 | tf_op jit(solution)/shard_map/all_to_all | solution.py:361

commit v2 on v1

--- a/solution.py
+++ b/solution.py
@@ -21,6 +21,7 @@
 OWN_UNROLL = 32
 HALO_UNROLL = 32
 PARTS = 8
+EDGE_PARTS = 2
 EDGES_MIB = 52.5
 SCALE = 1.0 / 625.0
 IN_VMEM = pl.BlockSpec(memory_space=pltpu.VMEM)
@@ -74,17 +75,22 @@
 
 
 def edges_kernel(obs, aux, dual, target, bottom, top, held, sems):
-    days, rows, _ = obs.shape
+    days, rows, columns = obs.shape
+    part = columns // EDGE_PARTS
     copies = []
-    for day in range(days):
+    for piece in range(EDGE_PARTS):
+        cols = pl.ds(piece * part, part)
         for k, array in enumerate((obs, aux, dual)):
-            copies.append(pltpu.make_async_copy(array.at[day], held.at[day, k], sems.at[day, k]))
+            copies.append(
+                pltpu.make_async_copy(array.at[:, :, cols], held.at[k, :, :, cols], sems.at[piece, k])
+            )
     for copy in copies:
         copy.start()
-    for day in range(days):
+    for piece in range(EDGE_PARTS):
+        cols = pl.ds(piece * part, part)
         for k in range(3):
-            copies[day * 3 + k].wait()
-        target[day] = held[day, 0] - held[day, 1] + held[day, 2]
+            copies[piece * 3 + k].wait()
+        target[:, :, cols] = held[0, :, :, cols] - held[1, :, :, cols] + held[2, :, :, cols]
     low = iota(top.shape, 0) < HALO
     last = rows - TILE
     top[...] = jnp.where(low, target[0, :TILE], pltpu.roll(target[1, :TILE], HALO, 0))
@@ -229,29 +235,27 @@
 def sums_kernel(obs, aux, dual, fitted, sums):
     blocks, days, rows, _ = fitted.shape
 
-    def body(group, carry):
-        primal, change = carry
-        for u in range(UNROLL):
-            j = group * UNROLL + u
-            cols = pl.ds(pl.multiple_of(j * LANES, LANES), LANES)
-            for day in range(days):
-                dual_now = dual[day, :, cols]
-                aux_new, dual_new = proximal(obs[day, :, cols], dual_now, fitted[j, day])
-                moved = dual_new - dual_now
-                primal += moved * moved
-                moved = aux_new - aux[day, :, cols]
-                change += moved * moved
-        return primal, change
-
     zero = jnp.zeros((rows, LANES), jnp.float32)
-    primal, change = lax.fori_loop(0, blocks // UNROLL, body, (zero, zero))
+    totals = [[zero, zero] for _ in range(4)]
+    for j in range(blocks):
+        cols = pl.ds(j * LANES, LANES)
+        for day in range(days):
+            total = totals[(j * days + day) % len(totals)]
+            dual_now = dual[day, :, cols]
+            aux_new, dual_new = proximal(obs[day, :, cols], dual_now, fitted[j, day])
+            moved = dual_new - dual_now
+            total[0] += moved * moved
+            moved = aux_new - aux[day, :, cols]
+            total[1] += moved * moved
+    primal = (totals[0][0] + totals[1][0]) + (totals[2][0] + totals[3][0])
+    change = (totals[0][1] + totals[1][1]) + (totals[2][1] + totals[3][1])
     primal = jnp.sum(primal, axis=0, keepdims=True)
     change = jnp.sum(change, axis=0, keepdims=True)
     half = LANES // 2
     both = jnp.where(
         iota((1, LANES), 1) < half, primal + pltpu.roll(primal, half, 1), change + pltpu.roll(change, half, 1)
     )
-    sums[...] = jnp.broadcast_to(both[None], sums.shape)
+    sums[...] = jnp.broadcast_to(both, sums.shape)
 
 
 def results_kernel(
@@ -298,7 +302,7 @@
 
 
 def norms_kernel(sums, primal, change):
-    row = jnp.sum(sums[...], axis=0)
+    row = jnp.sum(sums[...], axis=0, keepdims=True)
     half = iota(row.shape, 1) < LANES // 2
     primal[...] = jnp.sqrt(jnp.sum(jnp.where(half, row, 0.0), axis=1, keepdims=True))
     change[...] = PENALTY * jnp.sqrt(jnp.sum(jnp.where(half, 0.0, row), axis=1, keepdims=True))
@@ -319,7 +323,7 @@
         [IN_HBM] * 3,
         (IN_VMEM,) * 3,
         2.0,
-        [pltpu.VMEM((days, 3, rows, columns), jnp.float32), DMA((days, 3))],
+        [pltpu.VMEM((3, days, rows, columns), jnp.float32), DMA((EDGE_PARTS, 3))],
         EDGES_MIB,
     )(*state)
     above = lax.ppermute(bottom, "lat", [(i, (i + 1) % lat_count) for i in range(lat_count)])
@@ -340,7 +344,7 @@
     fitted = call(fitted_kernel, f32(all_days * rows, LANES), [IN_VMEM] * 2, IN_VMEM, 2.0)(smooth, to_fitted)
     fitted = lax.all_to_all(fitted.reshape(field.shape), "lon", 0, 0, tiled=True)
     devices = lat_count * lon_count
-    sums = call(sums_kernel, f32(devices, 1, LANES), [IN_VMEM] * 4, IN_VMEM, 1.0)(
+    sums = call(sums_kernel, f32(devices, LANES), [IN_VMEM] * 4, IN_VMEM, 1.0)(
         *state, fitted
     )
     coefficients, aux_next, dual_next = call(
@@ -358,7 +362,7 @@
         ],
     )(smooth, to_coefficients, observations, dual_state, fitted, sums)
     coefficients = coefficients.reshape(depth, rows, LANES)
-    sums = lax.all_to_all(sums, ("lat", "lon"), 0, 0, tiled=True)
+    sums = lax.all_to_all(sums.reshape(devices, 1, LANES), ("lat", "lon"), 0, 0, tiled=True).reshape(devices, LANES)
     primal, change = call(norms_kernel, (f32(1, 1), f32(1, 1)), [IN_VMEM], (IN_VMEM, IN_VMEM), 0.5)(sums)
     return (coefficients, aux_next, dual_next, primal.reshape(()), change.reshape(()))
 

time: 69.5 us -> 69.3 us (level)
  no operation moved by 1% of the time
where the time goes in v2:
time: 69.3 us; the launch traced here: 69 us
  blocking collectives  40.4 us (58%)
  Pallas kernels  10.9 us (16%)
  starting transfers between devices  10.5 us (15%)
  waiting for transfers between devices  6.53 us (9%)
  between operations  0.75 us (1%)
    all_to_all x1, blocking collectives, local(): lax.all_to_all(smooth, 'lon', 0, 0, tiled=True)  22.5 us
    all_to_all x1, blocking collectives, local(): lax.all_to_all(fitted.reshape(field.shape), 'lon', 0, 0, tiled=True)  17.9 us
    all_to_all x1, waiting for transfers between devices, local(): lax.all_to_all(sums.reshape(devices, 1, LANES), ('lat', 'lon'), 0, 0, til...  5.95 us
    all_to_all x1, starting transfers between devices, local(): lax.all_to_all(sums.reshape(devices, 1, LANES), ('lat', 'lon'), 0, 0, til...  5.76 us
    pallas_call x1, Pallas kernels, local(): call(results_kernel, (f32(depth * rows, LANES), slab, slab), [IN_VMEM] *...  3.65 us
    ppermute x1, starting transfers between devices, local(): lax.ppermute(bottom, 'lat', [(i, (i + 1) % lat_count) for i in range(lat_...  2.54 us
    ppermute x1, starting transfers between devices, local(): lax.ppermute(top, 'lat', [((i + 1) % lat_count, i) for i in range(lat_cou...  2.2 us
    pallas_call x1, Pallas kernels, local(): call(edges_kernel, (slab, tile, tile), [IN_HBM] * 3, (IN_VMEM,) * 3, 2.0,...  1.8 us
  transfers between devices with their start and end apart: 3, of which 2 were waited for; matrix products, arithmetic and copies ran while one was open for 0% of the time, Pallas kernels for 9%

profile of v2, /device:TPU:1, one launch (start us, length us, event | category | flops | bytes accessed | tf_op | source)
XLA Modules:
  0.0 69.0 jit_solution(7442739111697354216)
XLA Ops:
  0.6 0.0 copy-start.5
  0.6 1.8 %shard_map.101 = (f32[2,24,4096]{2,1,0:T(8,128)S(1)}, f32[8,4096]{1,0:T(8,128)S(1)}, f32[8,4096]{1,0:T(8,128)S(1)}) custom-call(f32[2,24,4096]{2,1,0:T(8,128)} %obs.5, f32[2,24,4096]{2,1,0:T(8,128)} %aux.3, f32[2,24,4096]{2,1,0:T(8,128)} %dual.5), custom_call_target="tpu_custom_call" | custom-call | flops 2000000000 | tf_op jit(solution)/shard_map/pallas_call | solution.py:320
  2.4 0.0 copy-start
  2.5 0.0 copy-start.4
  2.5 2.5 %collective-permute-start = (f32[8,4096]{1,0:T(8,128)S(1)}, f32[8,4096]{1,0:T(8,128)S(1)}, u32[]{:S(2)}, u32[]{:S(2)}) collective-permute-start(f32[8,4096]{1,0:T(8,128)S(1)} %get-tuple-element.16), channel_id=1, source_target_pairs={{0,32},{32,64},{64,96},{96,0},{1,33},{33,65},{65,97},{97,1},{2,34}... | collective-permute-start | bytes 393224 | tf_op jit(solution)/shard_map/ppermute | solution.py:329
  5.0 2.2 %collective-permute-start.1 = (f32[8,4096]{1,0:T(8,128)S(1)}, f32[8,4096]{1,0:T(8,128)S(1)}, u32[]{:S(2)}, u32[]{:S(2)}) collective-permute-start(f32[8,4096]{1,0:T(8,128)S(1)} %get-tuple-element.17), channel_id=1, source_target_pairs={{32,0},{64,32},{96,64},{0,96},{33,1},{65,33},{97,65},{1,97},{34,2}... | collective-permute-start | bytes 393224 | tf_op jit(solution)/shard_map/ppermute | solution.py:330
  7.2 0.0 copy-done.5
  7.2 1.5 %shard_map.102.own = f32[32,2,24,128]{3,2,1,0:T(8,128)S(1)} custom-call(f32[2,24,4096]{2,1,0:T(8,128)S(1)} %get-tuple-element.15.target, bf16[512,512]{1,0:T(8,128)(2,1)S(1)} %copy-done.5), custom_call_target="tpu_custom_call" | custom-call | flops 3000000000 | tf_op jit(solution)/shard_map/pallas_call | solution.py:332
  8.7 0.0 copy-done
  8.8 0.0 copy-done.4
  8.8 1.0 %shard_map.103 = (bf16[512,192]{1,0:T(8,128)(2,1)S(1)}, bf16[64,192]{1,0:T(8,128)(2,1)S(1)}) custom-call(f32[64,512]{1,0:T(8,128)S(1)} %copy-done.4, f32[512,512]{1,0:T(8,128)S(1)} %copy-done), custom_call_target="tpu_custom_call" | custom-call | flops 2000000000 | tf_op jit(solution)/shard_map/pallas_call | solution.py:333
  9.8 0.6 collective-permute-done.above
  10.4 0.0 collective-permute-done.1.below
  10.4 0.9 %shard_map.104 = f32[32,2,24,128]{3,2,1,0:T(8,128)S(1)} custom-call(f32[32,2,24,128]{3,2,1,0:T(8,128)S(1)} %shard_map.102.own, f32[8,4096]{1,0:T(8,128)S(1)} %collective-permute-done.above, f32[8,4096]{1,0:T(8,128)S(1)} %collective-permute-done.1.below, bf16[512,512]{1,0:T(8,128)(2,1)S(1)} %copy-done.5, bf16[64,192]{1,0:T(8,128)(2,1)S(1)} %get-tuple-element.18.after.matrix), custom_call_target="tpu_custom_call" | custom-call | flops 1500000000 | tf_op jit(solution)/shard_map/pallas_call | solution.py:340
  11.3 0.0 copy-start.1
  11.3 0.0 copy-start.2
  11.3 0.0 copy-start.3
  11.3 22.5 %all_to_all.15 = f32[32,2,24,128]{3,2,1,0:T(8,128)S(1)} all-to-all(f32[32,2,24,128]{3,2,1,0:T(8,128)S(1)} %shard_map.104), channel_id=1, replica_groups=mesh['lat'=4,'lon'=32] {'lon'}, dimensions={0} | all-to-all | bytes 1572864 | tf_op jit(solution)/shard_map/all_to_all | solution.py:343
  33.8 0.4 shard_map.105
  34.1 17.9 %all_to_all.16.fitted = f32[32,2,24,128]{3,2,1,0:T(8,128)S(1)} all-to-all(f32[32,2,24,128]{3,2,1,0:T(8,128)S(1)} %bitcast.11), channel_id=1, replica_groups=mesh['lat'=4,'lon'=32] {'lon'}, dimensions={0} | all-to-all | bytes 1572864 | tf_op jit(solution)/shard_map/all_to_all | solution.py:345
  52.0 0.0 copy-done.1
  52.0 0.0 copy-done.2
  52.0 0.0 copy-done.3
  52.0 1.0 %shard_map.106.after = f32[128,128]{1,0:T(8,128)} custom-call(f32[2,24,4096]{2,1,0:T(8,128)S(1)} %copy-done.2, f32[2,24,4096]{2,1,0:T(8,128)S(1)} %copy-done.1, f32[2,24,4096]{2,1,0:T(8,128)S(1)} %copy-done.3, f32[32,2,24,128]{3,2,1,0:T(8,128)S(1)} %all_to_all.16.fitted), custom_call_target="tpu_custom_call" | custom-call | flops 1000000000 | tf_op jit(solution)/shard_map/pallas_call | solution.py:347
  53.0 5.8 %all-to-all-start.2 = ((f32[128,1,128]{2,1,0:T(1,128)}), f32[128,1,128]{2,1,0:T(1,128)S(1)}, u32[]{:S(2)}, u32[]{:S(2)}) async-start(f32[128,1,128]{2,1,0:T(1,128)} %bitcast.4), calls=%async_computation.2 | async-start | bytes 131072 | tf_op jit(solution)/shard_map/all_to_all | solution.py:365
  58.8 3.7 %shard_map.107 = (f32[12288,128]{1,0:T(8,128)}, f32[2,24,4096]{2,1,0:T(8,128)}, f32[2,24,4096]{2,1,0:T(8,128)}) custom-call(f32[1536,128]{1,0:T(8,128)S(1)} %bitcast.10, bf16[512,192]{1,0:T(8,128)(2,1)S(1)} %get-tuple-element.19.matrix, f32[2,24,4096]{2,1,0:T(8,128)S(1)} %copy-done.2, f32[2,24,4096]{2,1,0:T(8,128)S(1)} %copy-done.3, ...), custom_call_target="tpu_custom_call" | custom-call | flops 5000000000 | tf_op jit(solution)/shard_map/pallas_call | solution.py:350
  62.5 5.9 %all-to-all-done.2 = f32[128,1,128]{2,1,0:T(1,128)S(1)} async-done(((f32[128,1,128]{2,1,0:T(1,128)}), f32[128,1,128]{2,1,0:T(1,128)S(1)}, u32[]{:S(2)}, u32[]{:S(2)}) %all-to-all-start.2) | async-done | bytes 65568 | tf_op jit(solution)/shard_map/all_to_all | solution.py:365
  68.4 0.6 shard_map.108
Async XLA Ops:
  0.6 6.6 %copy-start.5 = (bf16[512,512]{1,0:T(8,128)(2,1)S(1)}, bf16[512,512]{1,0:T(8,128)(2,1)}, u32[]{:S(2)}) copy-start(bf16[512,512]{1,0:T(8,128)(2,1)} %constant.2.clone.operator) | copy-start | bytes 1572868
  2.4 6.3 %copy-start = (f32[512,512]{1,0:T(8,128)S(1)}, f32[512,512]{1,0:T(8,128)}, u32[]{:S(2)}) copy-start(f32[512,512]{1,0:T(8,128)} %inverse_gram.1) | copy-start | bytes 3145732
  2.5 6.3 %copy-start.4 = (f32[64,512]{1,0:T(8,128)S(1)}, f32[64,512]{1,0:T(8,128)}, u32[]{:S(2)}) copy-start(f32[64,512]{1,0:T(8,128)} %predictors.1) | copy-start | bytes 393220
  2.5 7.9 %collective-permute-start = (f32[8,4096]{1,0:T(8,128)S(1)}, f32[8,4096]{1,0:T(8,128)S(1)}, u32[]{:S(2)}, u32[]{:S(2)}) collective-permute-start(f32[8,4096]{1,0:T(8,128)S(1)} %get-tuple-element.16), channel_id=1, source_target_pairs={{0,32},{32,64},{64,96},{96,0},{1,33},{33,65},{65,97},{97,1},{2,34}... | collective-permute-start | bytes 393224 | tf_op jit(solution)/shard_map/ppermute | solution.py:329
  5.0 5.3 %collective-permute-start.1 = (f32[8,4096]{1,0:T(8,128)S(1)}, f32[8,4096]{1,0:T(8,128)S(1)}, u32[]{:S(2)}, u32[]{:S(2)}) collective-permute-start(f32[8,4096]{1,0:T(8,128)S(1)} %get-tuple-element.17), channel_id=1, source_target_pairs={{32,0},{64,32},{96,64},{0,96},{33,1},{65,33},{97,65},{1,97},{34,2}... | collective-permute-start | bytes 393224 | tf_op jit(solution)/shard_map/ppermute | solution.py:330
  11.3 40.8 %copy-start.1 = (f32[2,24,4096]{2,1,0:T(8,128)S(1)}, f32[2,24,4096]{2,1,0:T(8,128)}, u32[]{:S(2)}) copy-start(f32[2,24,4096]{2,1,0:T(8,128)} %aux.3) | copy-start | bytes 2359300
  11.3 40.7 %copy-start.2 = (f32[2,24,4096]{2,1,0:T(8,128)S(1)}, f32[2,24,4096]{2,1,0:T(8,128)}, u32[]{:S(2)}) copy-start(f32[2,24,4096]{2,1,0:T(8,128)} %obs.5) | copy-start | bytes 2359300
  11.3 40.7 %copy-start.3 = (f32[2,24,4096]{2,1,0:T(8,128)S(1)}, f32[2,24,4096]{2,1,0:T(8,128)}, u32[]{:S(2)}) copy-start(f32[2,24,4096]{2,1,0:T(8,128)} %dual.5) | copy-start | bytes 2359300
  53.0 15.4 %all-to-all-start.2 = ((f32[128,1,128]{2,1,0:T(1,128)}), f32[128,1,128]{2,1,0:T(1,128)S(1)}, u32[]{:S(2)}, u32[]{:S(2)}) async-start(f32[128,1,128]{2,1,0:T(1,128)} %bitcast.4), calls=%async_computation.2 | async-start | bytes 131072 | tf_op jit(solution)/shard_map/all_to_all | solution.py:365

commit v3 on v2

--- a/solution.py
+++ b/solution.py
@@ -19,7 +19,6 @@
 TILE = 8
 UNROLL = 8
 OWN_UNROLL = 32
-HALO_UNROLL = 32
 PARTS = 8
 EDGE_PARTS = 2
 EDGES_MIB = 52.5
@@ -53,25 +52,36 @@
     return lax.broadcasted_iota(jnp.int32, shape, dim)
 
 
-def columns_operator():
+def columns_bands():
     powers = [np.array([1.0])]
     for _ in range(SWEEPS):
         powers.append(np.convolve(powers[-1], [1.0, 0.0, 1.0]))
     weights = [5.0 ** (SWEEPS - 1 - j) for j in range(SWEEPS)] + [1.0]
-    inner = np.zeros((LANES, SWEEPS, LANES))
-    outer = np.zeros((LANES, SWEEPS, LANES))
-    for k in range(SWEEPS):
-        band = np.zeros(2 * SWEEPS + 1)
+    bands = np.zeros((SWEEPS + 1, 2 * SWEEPS + 1))
+    for k in range(SWEEPS + 1):
         for j in range(k, SWEEPS + 1):
             reach = j - k
-            band[SWEEPS - reach : SWEEPS + reach + 1] += weights[j] * math.comb(j, k) * powers[reach]
+            bands[k, SWEEPS - reach : SWEEPS + reach + 1] += weights[j] * math.comb(j, k) * powers[reach]
+    return bands
+
+
+def distance_bands():
+    bands = columns_bands()
+    walks = [[math.comb(k, (k + d) // 2) * ((k + d) % 2 == 0) for k in range(SWEEPS + 1)] for d in range(1, SWEEPS)]
+    return np.array([sum(walks[d - 1][k] * bands[k] for k in range(d, SWEEPS + 1)) for d in range(1, SWEEPS)])
+
+
+def columns_operator(bands):
+    inner = np.zeros((LANES, len(bands), LANES))
+    outer = np.zeros((LANES, len(bands), LANES))
+    for k, band in enumerate(bands):
         for lane in range(LANES):
             for step in range(-SWEEPS, SWEEPS + 1):
                 source = lane + step
                 into = inner if 0 <= source < LANES else outer
                 into[source % LANES, k, lane] = band[SWEEPS + step]
-    inner, outer = (part.reshape(LANES, SWEEPS * LANES) for part in (inner, outer))
-    return np.concatenate([inner, inner, outer, outer], axis=0)
+    inner, outer = (part.reshape(LANES, len(bands) * LANES) for part in (inner, outer))
+    return jnp.asarray(np.concatenate([inner, inner, outer, outer], axis=0), jnp.bfloat16)
 
 
 def edges_kernel(obs, aux, dual, target, bottom, top, held, sems):
@@ -146,51 +156,32 @@
     blocks, days, rows, _ = own.shape
     row = iota((TILE, LANES), 0)
     low = row < HALO
-    begin, end = row == 0, row == TILE - 1
+    place = lax.rem(row, HALO)
     zero = jnp.zeros((TILE, LANES), jnp.float32)
     lat = lax.axis_index("lat")
     south_scale = jnp.where(lat < lat_count - 1, SCALE, 0.0)
     north_scale = jnp.where(lat > 0, SCALE, 0.0)
-
-    def spread(south, north):
-        return (
-            (jnp.where(low, pltpu.roll(north, HALO, 0), zero), jnp.where(low, zero, pltpu.roll(south, HALO, 0))),
-            (jnp.where(low, north, zero), jnp.where(low, zero, south)),
-        )
-
-    def body(group, carry):
-        start = group * HALO_UNROLL
-        held = []
-        for u in range(-1, HALO_UNROLL + 1):
-            j = lax.rem(start + u + blocks, blocks)
-            cols = pl.ds(pl.multiple_of(j * LANES, LANES), LANES)
-            held.append(jnp.concatenate([below[:, cols], above[:, cols]], axis=0))
-        parts = columns_part(held, operator)
-        for u in range(HALO_UNROLL):
-            at = u * 2 * TILE
-            now = spread(held[u + 1][:TILE], held[u + 1][TILE:])
-            for k in reversed(range(SWEEPS)):
-                cols = slice(k * LANES, (k + 1) * LANES)
-                part = spread(parts[at : at + TILE, cols], parts[at + TILE : at + 2 * TILE, cols])
-                now = tuple(
-                    tuple(
-                        jnp.where(begin, zero, pltpu.roll(now[day][side], 1, 0))
-                        + jnp.where(end, zero, pltpu.roll(now[day][side], TILE - 1, 0))
-                        + part[day][side]
-                        for side in range(2)
-                    )
-                    for day in range(days)
-                )
-            j = start + u
-            for day in range(days):
-                north = pltpu.roll(now[day][0], HALO, 0) * north_scale
-                south = pltpu.roll(now[day][1], HALO, 0) * south_scale
-                out[j, day, :TILE] = own[j, day, :TILE] + jnp.where(low, north, zero)
-                out[j, day, TILE : rows - TILE] = own[j, day, TILE : rows - TILE]
-                out[j, day, rows - TILE :] = own[j, day, rows - TILE :] + jnp.where(low, zero, south)
-        return carry
-
-    lax.fori_loop(0, blocks // HALO_UNROLL, body, 0)
+    held = []
+    for u in range(-1, blocks + 1):
+        cols = pl.ds((u % blocks) * LANES, LANES)
+        held.append(jnp.concatenate([below[:, cols], above[:, cols]], axis=0))
+    parts = columns_part(held, operator)
+    for j in range(blocks):
+        at = j * 2 * TILE
+        south = pltpu.roll(held[j + 1][:TILE], HALO, 0)
+        north = pltpu.roll(held[j + 1][TILE:], HALO, 0)
+        for d in range(1, HALO):
+            part = parts[at : at + 2 * TILE, (d - 1) * LANES : d * LANES]
+            south += jnp.where(place >= HALO - d, pltpu.roll(part[:TILE], TILE - d, 0), zero)
+            north += jnp.where(place < d, pltpu.roll(part[TILE:], d, 0), zero)
+        south = south * south_scale
+        north = north * north_scale
+        for day in range(days):
+            north_day = north if day == 0 else pltpu.roll(north, HALO, 0)
+            south_day = south if day == 0 else pltpu.roll(south, HALO, 0)
+            out[j, day, :TILE] = own[j, day, :TILE] + jnp.where(low, north_day, zero)
+            out[j, day, TILE : rows - TILE] = own[j, day, TILE : rows - TILE]
+            out[j, day, rows - TILE :] = own[j, day, rows - TILE :] + jnp.where(low, zero, south_day)
 
 
 def stack_left(matrix):
@@ -328,8 +319,9 @@
     )(*state)
     above = lax.ppermute(bottom, "lat", [(i, (i + 1) % lat_count) for i in range(lat_count)])
     below = lax.ppermute(top, "lat", [((i + 1) % lat_count, i) for i in range(lat_count)])
-    operator = jnp.asarray(columns_operator(), jnp.bfloat16)
-    own = call(functools.partial(own_kernel, lat_count), field, [IN_VMEM] * 2, IN_VMEM, 3.0)(target, operator)
+    own = call(functools.partial(own_kernel, lat_count), field, [IN_VMEM] * 2, IN_VMEM, 3.0)(
+        target, columns_operator(columns_bands()[:SWEEPS])
+    )
     to_coefficients, to_fitted = call(
         maps_kernel,
         (bf16(depth, 3 * all_days), bf16(all_days, 3 * all_days)),
@@ -338,7 +330,7 @@
         2.0,
     )(predictors, inverse_gram)
     smooth = call(functools.partial(halo_kernel, lat_count), field, [IN_VMEM] * 5, IN_VMEM, 1.5)(
-        own, above, below, operator, to_fitted
+        own, above, below, columns_operator(distance_bands()), to_fitted
     )
     smooth = lax.all_to_all(smooth, "lon", 0, 0, tiled=True).reshape(all_days * rows, LANES)
     fitted = call(fitted_kernel, f32(all_days * rows, LANES), [IN_VMEM] * 2, IN_VMEM, 2.0)(smooth, to_fitted)

time: 69.3 us -> 68.8 us (level)
  no operation moved by 1% of the time
where the time goes in v3:
time: 68.8 us; the launch traced here: 68.6 us
  blocking collectives  40.4 us (59%)
  starting transfers between devices  10.5 us (15%)
  Pallas kernels  10.4 us (15%)
  waiting for transfers between devices  6.53 us (9%)
  between operations  0.76 us (1%)
    all_to_all x1, blocking collectives, local(): lax.all_to_all(smooth, 'lon', 0, 0, tiled=True)  22.5 us
    all_to_all x1, blocking collectives, local(): lax.all_to_all(fitted.reshape(field.shape), 'lon', 0, 0, tiled=True)  17.9 us
    all_to_all x1, waiting for transfers between devices, local(): lax.all_to_all(sums.reshape(devices, 1, LANES), ('lat', 'lon'), 0, 0, til...  5.95 us
    all_to_all x1, starting transfers between devices, local(): lax.all_to_all(sums.reshape(devices, 1, LANES), ('lat', 'lon'), 0, 0, til...  5.76 us
    pallas_call x1, Pallas kernels, local(): call(results_kernel, (f32(depth * rows, LANES), slab, slab), [IN_VMEM] *...  3.65 us
    ppermute x1, starting transfers between devices, local(): lax.ppermute(bottom, 'lat', [(i, (i + 1) % lat_count) for i in range(lat_...  2.54 us
    ppermute x1, starting transfers between devices, local(): lax.ppermute(top, 'lat', [((i + 1) % lat_count, i) for i in range(lat_cou...  2.2 us
    pallas_call x1, Pallas kernels, local(): call(edges_kernel, (slab, tile, tile), [IN_HBM] * 3, (IN_VMEM,) * 3, 2.0,...  1.8 us
  transfers between devices with their start and end apart: 3, of which 2 were waited for; matrix products, arithmetic and copies ran while one was open for 0% of the time, Pallas kernels for 9%

profile of v3, /device:TPU:1, one launch (start us, length us, event | category | flops | bytes accessed | tf_op | source)
XLA Modules:
  0.0 68.6 jit_solution(9061960244513049400)
XLA Ops:
  0.6 0.0 copy-start.5
  0.6 1.8 %shard_map.110 = (f32[2,24,4096]{2,1,0:T(8,128)S(1)}, f32[8,4096]{1,0:T(8,128)S(1)}, f32[8,4096]{1,0:T(8,128)S(1)}) custom-call(f32[2,24,4096]{2,1,0:T(8,128)} %obs.5, f32[2,24,4096]{2,1,0:T(8,128)} %aux.3, f32[2,24,4096]{2,1,0:T(8,128)} %dual.5), custom_call_target="tpu_custom_call" | custom-call | flops 2000000000 | tf_op jit(solution)/shard_map/pallas_call | solution.py:311
  2.4 0.0 copy-start
  2.5 0.0 copy-start.4
  2.5 2.5 %collective-permute-start = (f32[8,4096]{1,0:T(8,128)S(1)}, f32[8,4096]{1,0:T(8,128)S(1)}, u32[]{:S(2)}, u32[]{:S(2)}) collective-permute-start(f32[8,4096]{1,0:T(8,128)S(1)} %get-tuple-element.16), channel_id=1, source_target_pairs={{0,32},{32,64},{64,96},{96,0},{1,33},{33,65},{65,97},{97,1},{2,34}... | collective-permute-start | bytes 393224 | tf_op jit(solution)/shard_map/ppermute | solution.py:320
  5.0 2.2 %collective-permute-start.1 = (f32[8,4096]{1,0:T(8,128)S(1)}, f32[8,4096]{1,0:T(8,128)S(1)}, u32[]{:S(2)}, u32[]{:S(2)}) collective-permute-start(f32[8,4096]{1,0:T(8,128)S(1)} %get-tuple-element.17), channel_id=1, source_target_pairs={{32,0},{64,32},{96,64},{0,96},{33,1},{65,33},{97,65},{1,97},{34,2}... | collective-permute-start | bytes 393224 | tf_op jit(solution)/shard_map/ppermute | solution.py:321
  7.2 0.0 copy-done.5
  7.2 1.5 %shard_map.111.own = f32[32,2,24,128]{3,2,1,0:T(8,128)S(1)} custom-call(f32[2,24,4096]{2,1,0:T(8,128)S(1)} %get-tuple-element.15.target, bf16[512,512]{1,0:T(8,128)(2,1)S(1)} %copy-done.5), custom_call_target="tpu_custom_call" | custom-call | flops 3000000000 | tf_op jit(solution)/shard_map/pallas_call | solution.py:322
  8.7 0.0 copy-done
  8.8 0.0 copy-done.4
  8.8 0.0 copy-start.6
  8.8 1.0 %shard_map.112 = (bf16[512,192]{1,0:T(8,128)(2,1)S(1)}, bf16[64,192]{1,0:T(8,128)(2,1)S(1)}) custom-call(f32[64,512]{1,0:T(8,128)S(1)} %copy-done.4, f32[512,512]{1,0:T(8,128)S(1)} %copy-done), custom_call_target="tpu_custom_call" | custom-call | flops 2000000000 | tf_op jit(solution)/shard_map/pallas_call | solution.py:325
  9.8 0.6 collective-permute-done.above
  10.4 0.0 collective-permute-done.1.below
  10.4 0.0 copy-done.6
  10.4 0.5 shard_map.113
  10.8 0.0 copy-start.1
  10.8 0.0 copy-start.2
  10.8 0.0 copy-start.3
  10.9 22.5 %all_to_all.15 = f32[32,2,24,128]{3,2,1,0:T(8,128)S(1)} all-to-all(f32[32,2,24,128]{3,2,1,0:T(8,128)S(1)} %shard_map.113), channel_id=1, replica_groups=mesh['lat'=4,'lon'=32] {'lon'}, dimensions={0} | all-to-all | bytes 1572864 | tf_op jit(solution)/shard_map/all_to_all | solution.py:335
  33.3 0.4 shard_map.114
  33.7 17.9 %all_to_all.16.fitted = f32[32,2,24,128]{3,2,1,0:T(8,128)S(1)} all-to-all(f32[32,2,24,128]{3,2,1,0:T(8,128)S(1)} %bitcast.11), channel_id=1, replica_groups=mesh['lat'=4,'lon'=32] {'lon'}, dimensions={0} | all-to-all | bytes 1572864 | tf_op jit(solution)/shard_map/all_to_all | solution.py:337
  51.6 0.0 copy-done.1
  51.6 0.0 copy-done.2
  51.6 0.0 copy-done.3
  51.6 1.0 %shard_map.115.after = f32[128,128]{1,0:T(8,128)} custom-call(f32[2,24,4096]{2,1,0:T(8,128)S(1)} %copy-done.2, f32[2,24,4096]{2,1,0:T(8,128)S(1)} %copy-done.1, f32[2,24,4096]{2,1,0:T(8,128)S(1)} %copy-done.3, f32[32,2,24,128]{3,2,1,0:T(8,128)S(1)} %all_to_all.16.fitted), custom_call_target="tpu_custom_call" | custom-call | flops 1000000000 | tf_op jit(solution)/shard_map/pallas_call | solution.py:339
  52.6 5.8 %all-to-all-start.2 = ((f32[128,1,128]{2,1,0:T(1,128)}), f32[128,1,128]{2,1,0:T(1,128)S(1)}, u32[]{:S(2)}, u32[]{:S(2)}) async-start(f32[128,1,128]{2,1,0:T(1,128)} %bitcast.4), calls=%async_computation.2 | async-start | bytes 131072 | tf_op jit(solution)/shard_map/all_to_all | solution.py:357
  58.4 3.6 %shard_map.116 = (f32[12288,128]{1,0:T(8,128)}, f32[2,24,4096]{2,1,0:T(8,128)}, f32[2,24,4096]{2,1,0:T(8,128)}) custom-call(f32[1536,128]{1,0:T(8,128)S(1)} %bitcast.10, bf16[512,192]{1,0:T(8,128)(2,1)S(1)} %get-tuple-element.19.matrix, f32[2,24,4096]{2,1,0:T(8,128)S(1)} %copy-done.2, f32[2,24,4096]{2,1,0:T(8,128)S(1)} %copy-done.3, ...), custom_call_target="tpu_custom_call" | custom-call | flops 5000000000 | tf_op jit(solution)/shard_map/pallas_call | solution.py:342
  62.0 6.0 %all-to-all-done.2 = f32[128,1,128]{2,1,0:T(1,128)S(1)} async-done(((f32[128,1,128]{2,1,0:T(1,128)}), f32[128,1,128]{2,1,0:T(1,128)S(1)}, u32[]{:S(2)}, u32[]{:S(2)}) %all-to-all-start.2) | async-done | bytes 65568 | tf_op jit(solution)/shard_map/all_to_all | solution.py:357
  68.0 0.6 shard_map.117
Async XLA Ops:
  0.6 6.6 %copy-start.5 = (bf16[512,512]{1,0:T(8,128)(2,1)S(1)}, bf16[512,512]{1,0:T(8,128)(2,1)}, u32[]{:S(2)}) copy-start(bf16[512,512]{1,0:T(8,128)(2,1)} %constant.4.clone.operator) | copy-start | bytes 1572868
  2.4 6.3 %copy-start = (f32[512,512]{1,0:T(8,128)S(1)}, f32[512,512]{1,0:T(8,128)}, u32[]{:S(2)}) copy-start(f32[512,512]{1,0:T(8,128)} %inverse_gram.1) | copy-start | bytes 3145732
  2.5 6.3 %copy-start.4 = (f32[64,512]{1,0:T(8,128)S(1)}, f32[64,512]{1,0:T(8,128)}, u32[]{:S(2)}) copy-start(f32[64,512]{1,0:T(8,128)} %predictors.1) | copy-start | bytes 393220
  2.5 7.9 %collective-permute-start = (f32[8,4096]{1,0:T(8,128)S(1)}, f32[8,4096]{1,0:T(8,128)S(1)}, u32[]{:S(2)}, u32[]{:S(2)}) collective-permute-start(f32[8,4096]{1,0:T(8,128)S(1)} %get-tuple-element.16), channel_id=1, source_target_pairs={{0,32},{32,64},{64,96},{96,0},{1,33},{33,65},{65,97},{97,1},{2,34}... | collective-permute-start | bytes 393224 | tf_op jit(solution)/shard_map/ppermute | solution.py:320
  5.0 5.3 %collective-permute-start.1 = (f32[8,4096]{1,0:T(8,128)S(1)}, f32[8,4096]{1,0:T(8,128)S(1)}, u32[]{:S(2)}, u32[]{:S(2)}) collective-permute-start(f32[8,4096]{1,0:T(8,128)S(1)} %get-tuple-element.17), channel_id=1, source_target_pairs={{32,0},{64,32},{96,64},{0,96},{33,1},{65,33},{97,65},{1,97},{34,2}... | collective-permute-start | bytes 393224 | tf_op jit(solution)/shard_map/ppermute | solution.py:321
  8.8 1.6 %copy-start.6 = (bf16[512,384]{1,0:T(8,128)(2,1)S(1)}, bf16[512,384]{1,0:T(8,128)(2,1)}, u32[]{:S(2)}) copy-start(bf16[512,384]{1,0:T(8,128)(2,1)} %constant.5.clone.operator) | copy-start | bytes 1179652
  10.8 40.8 %copy-start.1 = (f32[2,24,4096]{2,1,0:T(8,128)S(1)}, f32[2,24,4096]{2,1,0:T(8,128)}, u32[]{:S(2)}) copy-start(f32[2,24,4096]{2,1,0:T(8,128)} %aux.3) | copy-start | bytes 2359300
  10.8 40.7 %copy-start.2 = (f32[2,24,4096]{2,1,0:T(8,128)S(1)}, f32[2,24,4096]{2,1,0:T(8,128)}, u32[]{:S(2)}) copy-start(f32[2,24,4096]{2,1,0:T(8,128)} %obs.5) | copy-start | bytes 2359300
  10.8 40.7 %copy-start.3 = (f32[2,24,4096]{2,1,0:T(8,128)S(1)}, f32[2,24,4096]{2,1,0:T(8,128)}, u32[]{:S(2)}) copy-start(f32[2,24,4096]{2,1,0:T(8,128)} %dual.5) | copy-start | bytes 2359300
  52.6 15.4 %all-to-all-start.2 = ((f32[128,1,128]{2,1,0:T(1,128)}), f32[128,1,128]{2,1,0:T(1,128)S(1)}, u32[]{:S(2)}, u32[]{:S(2)}) async-start(f32[128,1,128]{2,1,0:T(1,128)} %bitcast.4), calls=%async_computation.2 | async-start | bytes 131072 | tf_op jit(solution)/shard_map/all_to_all | solution.py:357

commit v4 on v3

--- a/solution.py
+++ b/solution.py
@@ -20,8 +20,7 @@
 UNROLL = 8
 OWN_UNROLL = 32
 PARTS = 8
-EDGE_PARTS = 2
-EDGES_MIB = 52.5
+EDGES_MIB = 53.5
 SCALE = 1.0 / 625.0
 IN_VMEM = pl.BlockSpec(memory_space=pltpu.VMEM)
 IN_HBM = pl.BlockSpec(memory_space=pltpu.HBM)
@@ -84,27 +83,27 @@
     return jnp.asarray(np.concatenate([inner, inner, outer, outer], axis=0), jnp.bfloat16)
 
 
-def edges_kernel(obs, aux, dual, target, bottom, top, held, sems):
-    days, rows, columns = obs.shape
-    part = columns // EDGE_PARTS
+def edges_kernel(obs, aux, dual, bottom, top, held, sems):
+    last = obs.shape[1] - TILE
     copies = []
-    for piece in range(EDGE_PARTS):
-        cols = pl.ds(piece * part, part)
+    for side, row in enumerate((0, last)):
         for k, array in enumerate((obs, aux, dual)):
             copies.append(
-                pltpu.make_async_copy(array.at[:, :, cols], held.at[k, :, :, cols], sems.at[piece, k])
+                pltpu.make_async_copy(array.at[:, pl.ds(row, TILE), :], held.at[side, k], sems.at[side, k])
             )
     for copy in copies:
         copy.start()
-    for piece in range(EDGE_PARTS):
-        cols = pl.ds(piece * part, part)
-        for k in range(3):
-            copies[piece * 3 + k].wait()
-        target[:, :, cols] = held[0, :, :, cols] - held[1, :, :, cols] + held[2, :, :, cols]
     low = iota(top.shape, 0) < HALO
-    last = rows - TILE
-    top[...] = jnp.where(low, target[0, :TILE], pltpu.roll(target[1, :TILE], HALO, 0))
-    bottom[...] = jnp.where(low, pltpu.roll(target[1, last:], HALO, 0), target[0, last:])
+
+    def target(day, side):
+        return held[side, 0, day] - held[side, 1, day] + held[side, 2, day]
+
+    for copy in copies[:3]:
+        copy.wait()
+    top[...] = jnp.where(low, target(0, 0), pltpu.roll(target(1, 0), HALO, 0))
+    for copy in copies[3:]:
+        copy.wait()
+    bottom[...] = jnp.where(low, pltpu.roll(target(1, 1), HALO, 0), target(0, 1))
 
 
 def split(x):
@@ -121,7 +120,7 @@
     return jnp.dot(jnp.concatenate(stacked, axis=0), operator[...], preferred_element_type=jnp.float32)
 
 
-def own_kernel(lat_count, target, operator, out):
+def own_kernel(lat_count, obs, aux, dual, operator, out):
     blocks, days, rows, _ = out.shape
     lat = lax.axis_index("lat")
     total = rows + TILE
@@ -135,7 +134,8 @@
         for u in range(-1, OWN_UNROLL + 1):
             j = lax.rem(start + u + blocks, blocks)
             cols = pl.ds(pl.multiple_of(j * LANES, LANES), LANES)
-            held.append(jnp.concatenate([target[day, :, cols] for day in range(days)], axis=0))
+            target = [obs[day, :, cols] - aux[day, :, cols] + dual[day, :, cols] for day in range(days)]
+            held.append(jnp.concatenate(target, axis=0))
         parts = columns_part(held, operator)
         for u in range(OWN_UNROLL):
             for day in range(days):
@@ -308,19 +308,19 @@
     state = (observations, aux_state, dual_state)
     slab = f32(days, rows, columns)
     tile = f32(TILE, columns)
-    target, bottom, top = call(
+    bottom, top = call(
         edges_kernel,
-        (slab, tile, tile),
+        (tile, tile),
         [IN_HBM] * 3,
-        (IN_VMEM,) * 3,
+        (IN_VMEM,) * 2,
         2.0,
-        [pltpu.VMEM((3, days, rows, columns), jnp.float32), DMA((EDGE_PARTS, 3))],
+        [pltpu.VMEM((2, 3, days, TILE, columns), jnp.float32), DMA((2, 3))],
         EDGES_MIB,
     )(*state)
     above = lax.ppermute(bottom, "lat", [(i, (i + 1) % lat_count) for i in range(lat_count)])
     below = lax.ppermute(top, "lat", [((i + 1) % lat_count, i) for i in range(lat_count)])
-    own = call(functools.partial(own_kernel, lat_count), field, [IN_VMEM] * 2, IN_VMEM, 3.0)(
-        target, columns_operator(columns_bands()[:SWEEPS])
+    own = call(functools.partial(own_kernel, lat_count), field, [IN_VMEM] * 4, IN_VMEM, 3.0)(
+        *state, columns_operator(columns_bands()[:SWEEPS])
     )
     to_coefficients, to_fitted = call(
         maps_kernel,

time: 68.8 us -> 68.4 us (level)
  no operation moved by 1% of the time
where the time goes in v4:
time: 68.4 us; the launch traced here: 68.2 us
  blocking collectives  40.2 us (59%)
  starting transfers between devices  10.5 us (15%)
  Pallas kernels  10.2 us (15%)
  waiting for transfers between devices  6.52 us (10%)
  between operations  0.76 us (1%)
    all_to_all x1, blocking collectives, local(): lax.all_to_all(smooth, 'lon', 0, 0, tiled=True)  22.3 us
    all_to_all x1, blocking collectives, local(): lax.all_to_all(fitted.reshape(field.shape), 'lon', 0, 0, tiled=True)  17.9 us
    all_to_all x1, waiting for transfers between devices, local(): lax.all_to_all(sums.reshape(devices, 1, LANES), ('lat', 'lon'), 0, 0, til...  5.95 us
    all_to_all x1, starting transfers between devices, local(): lax.all_to_all(sums.reshape(devices, 1, LANES), ('lat', 'lon'), 0, 0, til...  5.76 us
    pallas_call x1, Pallas kernels, local(): call(results_kernel, (f32(depth * rows, LANES), slab, slab), [IN_VMEM] *...  3.65 us
    ppermute x1, starting transfers between devices, local(): lax.ppermute(bottom, 'lat', [(i, (i + 1) % lat_count) for i in range(lat_...  2.54 us
    ppermute x1, starting transfers between devices, local(): lax.ppermute(top, 'lat', [((i + 1) % lat_count, i) for i in range(lat_cou...  2.2 us
    pallas_call x1, Pallas kernels, local(): call(edges_kernel, (tile, tile), [IN_HBM] * 3, (IN_VMEM,) * 2, 2.0, [pltp...  1.58 us
  transfers between devices with their start and end apart: 3, of which 2 were waited for; matrix products, arithmetic and copies ran while one was open for 0% of the time, Pallas kernels for 9%

profile of v4, /device:TPU:1, one launch (start us, length us, event | category | flops | bytes accessed | tf_op | source)
XLA Modules:
  0.0 68.2 jit_solution(15974408382635323220)
XLA Ops:
  0.6 0.0 copy-start.5
  0.6 0.0 copy-start.2
  0.7 0.0 copy-start.1
  0.7 0.0 copy-start.3
  0.7 1.6 %shard_map.111 = (f32[8,4096]{1,0:T(8,128)S(1)}, f32[8,4096]{1,0:T(8,128)S(1)}) custom-call(f32[2,24,4096]{2,1,0:T(8,128)} %obs.7, f32[2,24,4096]{2,1,0:T(8,128)} %aux.5, f32[2,24,4096]{2,1,0:T(8,128)} %dual.7), custom_call_target="tpu_custom_call" | custom-call | flops 2000000000 | tf_op jit(solution)/shard_map/pallas_call | solution.py:311
  2.3 0.0 copy-start
  2.3 0.0 copy-start.4
  2.3 2.5 %collective-permute-start = (f32[8,4096]{1,0:T(8,128)S(1)}, f32[8,4096]{1,0:T(8,128)S(1)}, u32[]{:S(2)}, u32[]{:S(2)}) collective-permute-start(f32[8,4096]{1,0:T(8,128)S(1)} %get-tuple-element.14), channel_id=1, source_target_pairs={{0,32},{32,64},{64,96},{96,0},{1,33},{33,65},{65,97},{97,1},{2,34}... | collective-permute-start | bytes 393224 | tf_op jit(solution)/shard_map/ppermute | solution.py:320
  4.8 2.2 %collective-permute-start.1 = (f32[8,4096]{1,0:T(8,128)S(1)}, f32[8,4096]{1,0:T(8,128)S(1)}, u32[]{:S(2)}, u32[]{:S(2)}) collective-permute-start(f32[8,4096]{1,0:T(8,128)S(1)} %get-tuple-element.15), channel_id=1, source_target_pairs={{32,0},{64,32},{96,64},{0,96},{33,1},{65,33},{97,65},{1,97},{34,2}... | collective-permute-start | bytes 393224 | tf_op jit(solution)/shard_map/ppermute | solution.py:321
  7.0 0.0 copy-done.5
  7.0 0.0 copy-done.2
  7.0 0.0 copy-done.1
  7.0 0.0 copy-done.3
  7.0 1.5 %shard_map.110.own = f32[32,2,24,128]{3,2,1,0:T(8,128)S(1)} custom-call(f32[2,24,4096]{2,1,0:T(8,128)S(1)} %copy-done.2, f32[2,24,4096]{2,1,0:T(8,128)S(1)} %copy-done.1, f32[2,24,4096]{2,1,0:T(8,128)S(1)} %copy-done.3, bf16[512,512]{1,0:T(8,128)(2,1)S(1)} %copy-done.5), custom_call_target="tpu_custom_call" | custom-call | flops 3000000000 | tf_op jit(solution)/shard_map/pallas_call | solution.py:322
  8.6 0.0 copy-done
  8.6 0.0 copy-done.4
  8.6 0.0 copy-start.6
  8.6 1.0 %shard_map.112 = (bf16[512,192]{1,0:T(8,128)(2,1)S(1)}, bf16[64,192]{1,0:T(8,128)(2,1)S(1)}) custom-call(f32[64,512]{1,0:T(8,128)S(1)} %copy-done.4, f32[512,512]{1,0:T(8,128)S(1)} %copy-done), custom_call_target="tpu_custom_call" | custom-call | flops 2000000000 | tf_op jit(solution)/shard_map/pallas_call | solution.py:325
  9.6 0.6 collective-permute-done.above
  10.2 0.0 collective-permute-done.1.below
  10.2 0.0 copy-done.6
  10.2 0.5 shard_map.113
  10.6 22.3 %all_to_all.15 = f32[32,2,24,128]{3,2,1,0:T(8,128)S(1)} all-to-all(f32[32,2,24,128]{3,2,1,0:T(8,128)S(1)} %shard_map.113), channel_id=1, replica_groups=mesh['lat'=4,'lon'=32] {'lon'}, dimensions={0} | all-to-all | bytes 1572864 | tf_op jit(solution)/shard_map/all_to_all | solution.py:335
  33.0 0.4 shard_map.114
  33.3 17.9 %all_to_all.16.fitted = f32[32,2,24,128]{3,2,1,0:T(8,128)S(1)} all-to-all(f32[32,2,24,128]{3,2,1,0:T(8,128)S(1)} %bitcast.11), channel_id=1, replica_groups=mesh['lat'=4,'lon'=32] {'lon'}, dimensions={0} | all-to-all | bytes 1572864 | tf_op jit(solution)/shard_map/all_to_all | solution.py:337
  51.2 1.0 %shard_map.115.after = f32[128,128]{1,0:T(8,128)} custom-call(f32[2,24,4096]{2,1,0:T(8,128)S(1)} %copy-done.2, f32[2,24,4096]{2,1,0:T(8,128)S(1)} %copy-done.1, f32[2,24,4096]{2,1,0:T(8,128)S(1)} %copy-done.3, f32[32,2,24,128]{3,2,1,0:T(8,128)S(1)} %all_to_all.16.fitted), custom_call_target="tpu_custom_call" | custom-call | flops 1000000000 | tf_op jit(solution)/shard_map/pallas_call | solution.py:339
  52.2 5.8 %all-to-all-start.2 = ((f32[128,1,128]{2,1,0:T(1,128)}), f32[128,1,128]{2,1,0:T(1,128)S(1)}, u32[]{:S(2)}, u32[]{:S(2)}) async-start(f32[128,1,128]{2,1,0:T(1,128)} %bitcast.4), calls=%async_computation.2 | async-start | bytes 131072 | tf_op jit(solution)/shard_map/all_to_all | solution.py:357
  58.0 3.6 %shard_map.116 = (f32[12288,128]{1,0:T(8,128)}, f32[2,24,4096]{2,1,0:T(8,128)}, f32[2,24,4096]{2,1,0:T(8,128)}) custom-call(f32[1536,128]{1,0:T(8,128)S(1)} %bitcast.10, bf16[512,192]{1,0:T(8,128)(2,1)S(1)} %get-tuple-element.17.matrix, f32[2,24,4096]{2,1,0:T(8,128)S(1)} %copy-done.2, f32[2,24,4096]{2,1,0:T(8,128)S(1)} %copy-done.3, ...), custom_call_target="tpu_custom_call" | custom-call | flops 5000000000 | tf_op jit(solution)/shard_map/pallas_call | solution.py:342
  61.7 6.0 %all-to-all-done.2 = f32[128,1,128]{2,1,0:T(1,128)S(1)} async-done(((f32[128,1,128]{2,1,0:T(1,128)}), f32[128,1,128]{2,1,0:T(1,128)S(1)}, u32[]{:S(2)}, u32[]{:S(2)}) %all-to-all-start.2) | async-done | bytes 65568 | tf_op jit(solution)/shard_map/all_to_all | solution.py:357
  67.6 0.6 shard_map.117
Async XLA Ops:
  0.6 6.4 %copy-start.5 = (bf16[512,512]{1,0:T(8,128)(2,1)S(1)}, bf16[512,512]{1,0:T(8,128)(2,1)}, u32[]{:S(2)}) copy-start(bf16[512,512]{1,0:T(8,128)(2,1)} %constant.4.clone.operator) | copy-start | bytes 1572868
  0.6 6.4 %copy-start.2 = (f32[2,24,4096]{2,1,0:T(8,128)S(1)}, f32[2,24,4096]{2,1,0:T(8,128)}, u32[]{:S(2)}) copy-start(f32[2,24,4096]{2,1,0:T(8,128)} %obs.7) | copy-start | bytes 2359300
  0.7 6.4 %copy-start.1 = (f32[2,24,4096]{2,1,0:T(8,128)S(1)}, f32[2,24,4096]{2,1,0:T(8,128)}, u32[]{:S(2)}) copy-start(f32[2,24,4096]{2,1,0:T(8,128)} %aux.5) | copy-start | bytes 2359300
  0.7 6.4 %copy-start.3 = (f32[2,24,4096]{2,1,0:T(8,128)S(1)}, f32[2,24,4096]{2,1,0:T(8,128)}, u32[]{:S(2)}) copy-start(f32[2,24,4096]{2,1,0:T(8,128)} %dual.7) | copy-start | bytes 2359300
  2.3 6.3 %copy-start = (f32[512,512]{1,0:T(8,128)S(1)}, f32[512,512]{1,0:T(8,128)}, u32[]{:S(2)}) copy-start(f32[512,512]{1,0:T(8,128)} %inverse_gram.1) | copy-start | bytes 3145732
  2.3 6.3 %copy-start.4 = (f32[64,512]{1,0:T(8,128)S(1)}, f32[64,512]{1,0:T(8,128)}, u32[]{:S(2)}) copy-start(f32[64,512]{1,0:T(8,128)} %predictors.1) | copy-start | bytes 393220
  2.3 7.9 %collective-permute-start = (f32[8,4096]{1,0:T(8,128)S(1)}, f32[8,4096]{1,0:T(8,128)S(1)}, u32[]{:S(2)}, u32[]{:S(2)}) collective-permute-start(f32[8,4096]{1,0:T(8,128)S(1)} %get-tuple-element.14), channel_id=1, source_target_pairs={{0,32},{32,64},{64,96},{96,0},{1,33},{33,65},{65,97},{97,1},{2,34}... | collective-permute-start | bytes 393224 | tf_op jit(solution)/shard_map/ppermute | solution.py:320
  4.8 5.3 %collective-permute-start.1 = (f32[8,4096]{1,0:T(8,128)S(1)}, f32[8,4096]{1,0:T(8,128)S(1)}, u32[]{:S(2)}, u32[]{:S(2)}) collective-permute-start(f32[8,4096]{1,0:T(8,128)S(1)} %get-tuple-element.15), channel_id=1, source_target_pairs={{32,0},{64,32},{96,64},{0,96},{33,1},{65,33},{97,65},{1,97},{34,2}... | collective-permute-start | bytes 393224 | tf_op jit(solution)/shard_map/ppermute | solution.py:321
  8.6 1.6 %copy-start.6 = (bf16[512,384]{1,0:T(8,128)(2,1)S(1)}, bf16[512,384]{1,0:T(8,128)(2,1)}, u32[]{:S(2)}) copy-start(bf16[512,384]{1,0:T(8,128)(2,1)} %constant.5.clone.operator) | copy-start | bytes 1179652
  52.2 15.4 %all-to-all-start.2 = ((f32[128,1,128]{2,1,0:T(1,128)}), f32[128,1,128]{2,1,0:T(1,128)S(1)}, u32[]{:S(2)}, u32[]{:S(2)}) async-start(f32[128,1,128]{2,1,0:T(1,128)} %bitcast.4), calls=%async_computation.2 | async-start | bytes 131072 | tf_op jit(solution)/shard_map/all_to_all | solution.py:357

commit v5 on v4

--- a/solution.py
+++ b/solution.py
@@ -83,7 +83,7 @@
     return jnp.asarray(np.concatenate([inner, inner, outer, outer], axis=0), jnp.bfloat16)
 
 
-def edges_kernel(obs, aux, dual, bottom, top, held, sems):
+def edges_kernel(obs, aux, dual, first, second, held, sems):
     last = obs.shape[1] - TILE
     copies = []
     for side, row in enumerate((0, last)):
@@ -93,17 +93,20 @@
             )
     for copy in copies:
         copy.start()
-    low = iota(top.shape, 0) < HALO
+    low = iota(first.shape, 0) < HALO
+    even = lax.rem(lax.axis_index("lat"), 2) == 0
 
     def target(day, side):
         return held[side, 0, day] - held[side, 1, day] + held[side, 2, day]
 
     for copy in copies[:3]:
         copy.wait()
-    top[...] = jnp.where(low, target(0, 0), pltpu.roll(target(1, 0), HALO, 0))
+    top = jnp.where(low, target(0, 0), pltpu.roll(target(1, 0), HALO, 0))
     for copy in copies[3:]:
         copy.wait()
-    bottom[...] = jnp.where(low, pltpu.roll(target(1, 1), HALO, 0), target(0, 1))
+    bottom = jnp.where(low, pltpu.roll(target(1, 1), HALO, 0), target(0, 1))
+    first[...] = jnp.where(even, bottom, top)
+    second[...] = jnp.where(even, top, bottom)
 
 
 def split(x):
@@ -152,19 +155,21 @@
     lax.fori_loop(0, blocks // OWN_UNROLL, body, 0)
 
 
-def halo_kernel(lat_count, own, above, below, operator, after, out):
+def halo_kernel(lat_count, own, second, first, operator, after, out):
     blocks, days, rows, _ = own.shape
     row = iota((TILE, LANES), 0)
     low = row < HALO
     place = lax.rem(row, HALO)
     zero = jnp.zeros((TILE, LANES), jnp.float32)
     lat = lax.axis_index("lat")
+    even = lax.rem(lat, 2) == 0
     south_scale = jnp.where(lat < lat_count - 1, SCALE, 0.0)
     north_scale = jnp.where(lat > 0, SCALE, 0.0)
     held = []
     for u in range(-1, blocks + 1):
         cols = pl.ds((u % blocks) * LANES, LANES)
-        held.append(jnp.concatenate([below[:, cols], above[:, cols]], axis=0))
+        one, two = first[:, cols], second[:, cols]
+        held.append(jnp.concatenate([jnp.where(even, one, two), jnp.where(even, two, one)], axis=0))
     parts = columns_part(held, operator)
     for j in range(blocks):
         at = j * 2 * TILE
@@ -189,15 +194,13 @@
     return jnp.concatenate([high, low, high], axis=1)
 
 
-def stack_right(matrix):
-    high, low = split(matrix)
-    return jnp.concatenate([high, high, low], axis=0)
-
-
 def maps_kernel(predictors, inverse_gram, to_coefficients, to_fitted):
     scores = predictors[...]
-    direct = jnp.dot(stack_left(inverse_gram[...]), stack_right(scores.T), preferred_element_type=jnp.float32)
-    back = jnp.dot(stack_left(scores), stack_right(direct), preferred_element_type=jnp.float32)
+    contract = (((1,), (1,)), ((), ()))
+    direct = lax.dot_general(
+        inverse_gram[...], scores, contract, precision=HIGHEST, preferred_element_type=jnp.float32
+    )
+    back = jnp.dot(scores, direct, precision=HIGHEST, preferred_element_type=jnp.float32)
     to_coefficients[...] = stack_left(direct)
     to_fitted[...] = stack_left(back)
 
@@ -262,6 +265,21 @@
         copies.append(pltpu.make_async_copy(source, target, sems.at[k]))
         copies[-1].start(priority=k % 2)
 
+    for day in range(days):
+
+        def body(group, carry):
+            for u in range(UNROLL):
+                j = group * UNROLL + u
+                cols = pl.ds(pl.multiple_of(j * LANES, LANES), LANES)
+                aux_new, dual_new = proximal(obs[day, :, cols], dual[day, :, cols], fitted[j, day])
+                aux_held[day, :, cols] = aux_new
+                dual_held[day, :, cols] = dual_new
+            return carry
+
+        lax.fori_loop(0, blocks // UNROLL, body, 0)
+        send(aux_held.at[day], aux_next.at[day], PARTS + day)
+        send(dual_held.at[day], dual_next.at[day], PARTS + days + day)
+
     for r, right in pairs(smooth, rows, days_all):
         stacked[r // 2] = right
     for k in range(PARTS):
@@ -273,21 +291,6 @@
                 held[pl.ds(k * part * rows + r + i, part, stride=rows), :] = both[:, i * LANES : (i + 1) * LANES]
         span = pl.ds(k * part * rows, part * rows)
         send(held.at[span], coefficients.at[span], k)
-
-    for day in range(days):
-
-        def body(group, carry):
-            for u in range(UNROLL):
-                j = group * UNROLL + u
-                cols = pl.ds(pl.multiple_of(j * LANES, LANES), LANES)
-                aux_new, dual_new = proximal(obs[day, :, cols], dual[day, :, cols], fitted[j, day])
-                aux_held[day, :, cols] = aux_new
-                dual_held[day, :, cols] = dual_new
-            return carry
-
-        lax.fori_loop(0, blocks // UNROLL, body, 0)
-        send(aux_held.at[day], aux_next.at[day], PARTS + day)
-        send(dual_held.at[day], dual_next.at[day], PARTS + days + day)
     for copy in copies:
         copy.wait()
 
@@ -308,7 +311,7 @@
     state = (observations, aux_state, dual_state)
     slab = f32(days, rows, columns)
     tile = f32(TILE, columns)
-    bottom, top = call(
+    first, second = call(
         edges_kernel,
         (tile, tile),
         [IN_HBM] * 3,
@@ -317,8 +320,8 @@
         [pltpu.VMEM((2, 3, days, TILE, columns), jnp.float32), DMA((2, 3))],
         EDGES_MIB,
     )(*state)
-    above = lax.ppermute(bottom, "lat", [(i, (i + 1) % lat_count) for i in range(lat_count)])
-    below = lax.ppermute(top, "lat", [((i + 1) % lat_count, i) for i in range(lat_count)])
+    first = lax.ppermute(first, "lat", [(i, i ^ 1) for i in range(lat_count)])
+    second = lax.ppermute(second, "lat", [(i, i ^ 3) for i in range(lat_count)])
     own = call(functools.partial(own_kernel, lat_count), field, [IN_VMEM] * 4, IN_VMEM, 3.0)(
         *state, columns_operator(columns_bands()[:SWEEPS])
     )
@@ -330,7 +333,7 @@
         2.0,
     )(predictors, inverse_gram)
     smooth = call(functools.partial(halo_kernel, lat_count), field, [IN_VMEM] * 5, IN_VMEM, 1.5)(
-        own, above, below, columns_operator(distance_bands()), to_fitted
+        own, second, first, columns_operator(distance_bands()), to_fitted
     )
     smooth = lax.all_to_all(smooth, "lon", 0, 0, tiled=True).reshape(all_days * rows, LANES)
     fitted = call(fitted_kernel, f32(all_days * rows, LANES), [IN_VMEM] * 2, IN_VMEM, 2.0)(smooth, to_fitted)

time: 68.4 us -> 68.4 us (level)
  starting transfers between devices: 10.5 us -> 8.88 us
  blocking collectives: 40.2 us -> 40.9 us
    all_to_all x1, starting transfers between devices: 5.76 us -> 4.21 us  [local(): lax.all_to_all(sums.reshape(devices, 1, LANES), ('lat', 'lon'), 0, 0, til...]
  transfers between devices with their start and end apart: 3 -> 3, of which waited for: 2 -> 3; matrix products, arithmetic and copies ran while one was open for 0% -> 0% of each run, Pallas kernels for 9% -> 9%
where the time goes in v5:
time: 68.4 us; the launch traced here: 68.2 us
  blocking collectives  40.9 us (60%)
  Pallas kernels  10.5 us (15%)
  starting transfers between devices  8.88 us (13%)
  waiting for transfers between devices  7.16 us (10%)
  between operations  0.77 us (1%)
    all_to_all x1, blocking collectives, local(): lax.all_to_all(smooth, 'lon', 0, 0, tiled=True)  23 us
    all_to_all x1, blocking collectives, local(): lax.all_to_all(fitted.reshape(field.shape), 'lon', 0, 0, tiled=True)  17.9 us
    all_to_all x1, waiting for transfers between devices, local(): lax.all_to_all(sums.reshape(devices, 1, LANES), ('lat', 'lon'), 0, 0, til...  6.1 us
    ppermute x1, starting transfers between devices, local(): second = lax.ppermute(second, 'lat', [(i, i ^ 3) for i in range(lat_count)])  4.67 us
    all_to_all x1, starting transfers between devices, local(): lax.all_to_all(sums.reshape(devices, 1, LANES), ('lat', 'lon'), 0, 0, til...  4.21 us
    pallas_call x1, Pallas kernels, local(): call(results_kernel, (f32(depth * rows, LANES), slab, slab), [IN_VMEM] *...  3.5 us
    pallas_call x1, Pallas kernels, local(): call(edges_kernel, (tile, tile), [IN_HBM] * 3, (IN_VMEM,) * 2, 2.0, [pltp...  1.59 us
    pallas_call x1, Pallas kernels, local(): call(functools.partial(own_kernel, lat_count), field, [IN_VMEM] * 4, IN_V...  1.52 us
  transfers between devices with their start and end apart: 3, of which 3 were waited for; matrix products, arithmetic and copies ran while one was open for 0% of the time, Pallas kernels for 9%

profile of v5, /device:TPU:1, one launch (start us, length us, event | category | flops | bytes accessed | tf_op | source)
XLA Modules:
  0.0 68.2 jit_solution(13049935226309209489)
XLA Ops:
  0.6 0.0 copy-start.5
  0.6 0.0 copy-start.2
  0.7 0.0 copy-start.1
  0.7 0.0 copy-start.3
  0.7 1.6 %shard_map.111 = (f32[8,4096]{1,0:T(8,128)S(1)}, f32[8,4096]{1,0:T(8,128)S(1)}) custom-call(f32[2,24,4096]{2,1,0:T(8,128)} %obs.7, f32[2,24,4096]{2,1,0:T(8,128)} %aux.5, f32[2,24,4096]{2,1,0:T(8,128)} %dual.7), custom_call_target="tpu_custom_call" | custom-call | flops 2000000000 | tf_op jit(solution)/shard_map/pallas_call | solution.py:314
  2.3 0.0 copy-start
  2.3 0.0 copy-start.4
  2.3 4.7 %collective-permute-start = (f32[8,4096]{1,0:T(8,128)S(1)}, f32[8,4096]{1,0:T(8,128)S(1)}, u32[]{:S(2)}, u32[]{:S(2)}) collective-permute-start(f32[8,4096]{1,0:T(8,128)S(1)} %get-tuple-element.14), channel_id=1, source_target_pairs={{0,96},{32,64},{64,32},{96,0},{1,97},{33,65},{65,33},{97,1},{2,98}... | collective-permute-start | bytes 393224 | tf_op jit(solution)/shard_map/ppermute | solution.py:324
  7.0 0.0 collective-permute-start.1
  7.0 0.0 copy-done.5
  7.0 0.0 copy-done.2
  7.0 0.0 copy-done.1
  7.0 0.0 copy-done.3
  7.0 1.5 %shard_map.110.own = f32[32,2,24,128]{3,2,1,0:T(8,128)S(1)} custom-call(f32[2,24,4096]{2,1,0:T(8,128)S(1)} %copy-done.2, f32[2,24,4096]{2,1,0:T(8,128)S(1)} %copy-done.1, f32[2,24,4096]{2,1,0:T(8,128)S(1)} %copy-done.3, bf16[512,512]{1,0:T(8,128)(2,1)S(1)} %copy-done.5), custom_call_target="tpu_custom_call" | custom-call | flops 3000000000 | tf_op jit(solution)/shard_map/pallas_call | solution.py:325
  8.5 0.0 copy-done
  8.5 0.0 copy-done.4
  8.5 0.0 copy-start.6
  8.6 1.4 %shard_map.112 = (bf16[512,192]{1,0:T(8,128)(2,1)S(1)}, bf16[64,192]{1,0:T(8,128)(2,1)S(1)}) custom-call(f32[64,512]{1,0:T(8,128)S(1)} %copy-done.4, f32[512,512]{1,0:T(8,128)S(1)} %copy-done), custom_call_target="tpu_custom_call" | custom-call | flops 2000000000 | tf_op jit(solution)/shard_map/pallas_call | solution.py:328
  10.0 0.2 collective-permute-done.second
  10.2 0.8 %collective-permute-done.1.first = f32[8,4096]{1,0:T(8,128)S(1)} collective-permute-done((f32[8,4096]{1,0:T(8,128)S(1)}, f32[8,4096]{1,0:T(8,128)S(1)}, u32[]{:S(2)}, u32[]{:S(2)}) %collective-permute-start.1) | collective-permute-done | bytes 131104 | tf_op jit(solution)/shard_map/ppermute | solution.py:323
  11.0 0.0 copy-done.6
  11.0 0.5 shard_map.113
  11.5 23.0 %all_to_all.15 = f32[32,2,24,128]{3,2,1,0:T(8,128)S(1)} all-to-all(f32[32,2,24,128]{3,2,1,0:T(8,128)S(1)} %shard_map.113), channel_id=1, replica_groups=mesh['lat'=4,'lon'=32] {'lon'}, dimensions={0} | all-to-all | bytes 1572864 | tf_op jit(solution)/shard_map/all_to_all | solution.py:338
  34.5 0.4 shard_map.114
  34.8 17.9 %all_to_all.16.fitted = f32[32,2,24,128]{3,2,1,0:T(8,128)S(1)} all-to-all(f32[32,2,24,128]{3,2,1,0:T(8,128)S(1)} %bitcast.11), channel_id=1, replica_groups=mesh['lat'=4,'lon'=32] {'lon'}, dimensions={0} | all-to-all | bytes 1572864 | tf_op jit(solution)/shard_map/all_to_all | solution.py:340
  52.7 1.0 %shard_map.115.after = f32[128,128]{1,0:T(8,128)} custom-call(f32[2,24,4096]{2,1,0:T(8,128)S(1)} %copy-done.2, f32[2,24,4096]{2,1,0:T(8,128)S(1)} %copy-done.1, f32[2,24,4096]{2,1,0:T(8,128)S(1)} %copy-done.3, f32[32,2,24,128]{3,2,1,0:T(8,128)S(1)} %all_to_all.16.fitted), custom_call_target="tpu_custom_call" | custom-call | flops 1000000000 | tf_op jit(solution)/shard_map/pallas_call | solution.py:342
  53.7 4.2 %all-to-all-start.2 = ((f32[128,1,128]{2,1,0:T(1,128)}), f32[128,1,128]{2,1,0:T(1,128)S(1)}, u32[]{:S(2)}, u32[]{:S(2)}) async-start(f32[128,1,128]{2,1,0:T(1,128)} %bitcast.4), calls=%async_computation.2 | async-start | bytes 131072 | tf_op jit(solution)/shard_map/all_to_all | solution.py:360
  57.9 3.5 %shard_map.116 = (f32[12288,128]{1,0:T(8,128)}, f32[2,24,4096]{2,1,0:T(8,128)}, f32[2,24,4096]{2,1,0:T(8,128)}) custom-call(f32[1536,128]{1,0:T(8,128)S(1)} %bitcast.10, bf16[512,192]{1,0:T(8,128)(2,1)S(1)} %get-tuple-element.17.matrix, f32[2,24,4096]{2,1,0:T(8,128)S(1)} %copy-done.2, f32[2,24,4096]{2,1,0:T(8,128)S(1)} %copy-done.3, ...), custom_call_target="tpu_custom_call" | custom-call | flops 5000000000 | tf_op jit(solution)/shard_map/pallas_call | solution.py:345
  61.4 6.1 %all-to-all-done.2 = f32[128,1,128]{2,1,0:T(1,128)S(1)} async-done(((f32[128,1,128]{2,1,0:T(1,128)}), f32[128,1,128]{2,1,0:T(1,128)S(1)}, u32[]{:S(2)}, u32[]{:S(2)}) %all-to-all-start.2) | async-done | bytes 65568 | tf_op jit(solution)/shard_map/all_to_all | solution.py:360
  67.5 0.6 shard_map.117
Async XLA Ops:
  0.6 6.3 %copy-start.5 = (bf16[512,512]{1,0:T(8,128)(2,1)S(1)}, bf16[512,512]{1,0:T(8,128)(2,1)}, u32[]{:S(2)}) copy-start(bf16[512,512]{1,0:T(8,128)(2,1)} %constant.4.clone.operator) | copy-start | bytes 1572868
  0.6 6.3 %copy-start.2 = (f32[2,24,4096]{2,1,0:T(8,128)S(1)}, f32[2,24,4096]{2,1,0:T(8,128)}, u32[]{:S(2)}) copy-start(f32[2,24,4096]{2,1,0:T(8,128)} %obs.7) | copy-start | bytes 2359300
  0.7 6.3 %copy-start.1 = (f32[2,24,4096]{2,1,0:T(8,128)S(1)}, f32[2,24,4096]{2,1,0:T(8,128)}, u32[]{:S(2)}) copy-start(f32[2,24,4096]{2,1,0:T(8,128)} %aux.5) | copy-start | bytes 2359300
  0.7 6.3 %copy-start.3 = (f32[2,24,4096]{2,1,0:T(8,128)S(1)}, f32[2,24,4096]{2,1,0:T(8,128)}, u32[]{:S(2)}) copy-start(f32[2,24,4096]{2,1,0:T(8,128)} %dual.7) | copy-start | bytes 2359300
  2.3 6.3 %copy-start = (f32[512,512]{1,0:T(8,128)S(1)}, f32[512,512]{1,0:T(8,128)}, u32[]{:S(2)}) copy-start(f32[512,512]{1,0:T(8,128)} %inverse_gram.1) | copy-start | bytes 3145732
  2.3 6.3 %copy-start.4 = (f32[64,512]{1,0:T(8,128)S(1)}, f32[64,512]{1,0:T(8,128)}, u32[]{:S(2)}) copy-start(f32[64,512]{1,0:T(8,128)} %predictors.1) | copy-start | bytes 393220
  2.3 7.9 %collective-permute-start = (f32[8,4096]{1,0:T(8,128)S(1)}, f32[8,4096]{1,0:T(8,128)S(1)}, u32[]{:S(2)}, u32[]{:S(2)}) collective-permute-start(f32[8,4096]{1,0:T(8,128)S(1)} %get-tuple-element.14), channel_id=1, source_target_pairs={{0,96},{32,64},{64,32},{96,0},{1,97},{33,65},{65,33},{97,1},{2,98}... | collective-permute-start | bytes 393224 | tf_op jit(solution)/shard_map/ppermute | solution.py:324
  7.0 4.1 %collective-permute-start.1 = (f32[8,4096]{1,0:T(8,128)S(1)}, f32[8,4096]{1,0:T(8,128)S(1)}, u32[]{:S(2)}, u32[]{:S(2)}) collective-permute-start(f32[8,4096]{1,0:T(8,128)S(1)} %get-tuple-element.15), channel_id=1, source_target_pairs={{0,32},{32,0},{64,96},{96,64},{1,33},{33,1},{65,97},{97,65},{2,34}... | collective-permute-start | bytes 393224 | tf_op jit(solution)/shard_map/ppermute | solution.py:323
  8.5 2.5 %copy-start.6 = (bf16[512,384]{1,0:T(8,128)(2,1)S(1)}, bf16[512,384]{1,0:T(8,128)(2,1)}, u32[]{:S(2)}) copy-start(bf16[512,384]{1,0:T(8,128)(2,1)} %constant.5.clone.operator) | copy-start | bytes 1179652
  53.7 13.8 %all-to-all-start.2 = ((f32[128,1,128]{2,1,0:T(1,128)}), f32[128,1,128]{2,1,0:T(1,128)S(1)}, u32[]{:S(2)}, u32[]{:S(2)}) async-start(f32[128,1,128]{2,1,0:T(1,128)} %bitcast.4), calls=%async_computation.2 | async-start | bytes 131072 | tf_op jit(solution)/shard_map/all_to_all | solution.py:360

commit v6 on v5

--- a/solution.py
+++ b/solution.py
@@ -25,6 +25,17 @@
 IN_VMEM = pl.BlockSpec(memory_space=pltpu.VMEM)
 IN_HBM = pl.BlockSpec(memory_space=pltpu.HBM)
 DMA = pltpu.SemaphoreType.DMA
+
+
+def middle_pairs(lat_count, lon_count):
+    pairs = []
+    for lat in range(lat_count):
+        for lon in range(lon_count):
+            other = (lat + 1 if lat % 2 else lat - 1, lon)
+            if not 0 <= other[0] < lat_count:
+                other = (lat, lon ^ 1)
+            pairs.append((lat * lon_count + lon, other[0] * lon_count + other[1]))
+    return pairs
 
 
 def f32(*shape):
@@ -321,7 +332,7 @@
         EDGES_MIB,
     )(*state)
     first = lax.ppermute(first, "lat", [(i, i ^ 1) for i in range(lat_count)])
-    second = lax.ppermute(second, "lat", [(i, i ^ 3) for i in range(lat_count)])
+    second = lax.ppermute(second, ("lat", "lon"), middle_pairs(lat_count, lon_count))
     own = call(functools.partial(own_kernel, lat_count), field, [IN_VMEM] * 4, IN_VMEM, 3.0)(
         *state, columns_operator(columns_bands()[:SWEEPS])
     )

time: 68.4 us -> 67.9 us (level)
  waiting for transfers between devices: 7.16 us -> 6.1 us
  starting transfers between devices: 8.88 us -> 9.83 us
    ppermute x1, starting transfers between devices: 4.67 us -> 1.5 us  [local(): lax.ppermute(second, ('lat', 'lon'), middle_pairs(lat_count, lon_count))]
    ppermute x1, starting transfers between devices: 0.01 us -> 2.68 us  [local(): first = lax.ppermute(first, 'lat', [(i, i ^ 1) for i in range(lat_count)])]
    all_to_all x1, starting transfers between devices: 4.21 us -> 5.65 us  [local(): lax.all_to_all(sums.reshape(devices, 1, LANES), ('lat', 'lon'), 0, 0, til...]
    ppermute x1, waiting for transfers between devices: 0.83 us -> 0.01 us  [local(): first = lax.ppermute(first, 'lat', [(i, i ^ 1) for i in range(lat_count)])]
  transfers between devices with their start and end apart: 3 -> 3, of which waited for: 3 -> 1; matrix products, arithmetic and copies ran while one was open for 0% -> 0% of each run, Pallas kernels for 9% -> 10%
where the time goes in v6:
time: 67.9 us; the launch traced here: 67.6 us
  blocking collectives  40.4 us (59%)
  Pallas kernels  10.5 us (15%)
  starting transfers between devices  9.83 us (14%)
  waiting for transfers between devices  6.1 us (9%)
  between operations  0.77 us (1%)
    all_to_all x1, blocking collectives, local(): lax.all_to_all(smooth, 'lon', 0, 0, tiled=True)  22.6 us
    all_to_all x1, blocking collectives, local(): lax.all_to_all(fitted.reshape(field.shape), 'lon', 0, 0, tiled=True)  17.9 us
    all_to_all x1, waiting for transfers between devices, local(): lax.all_to_all(sums.reshape(devices, 1, LANES), ('lat', 'lon'), 0, 0, til...  6.09 us
    all_to_all x1, starting transfers between devices, local(): lax.all_to_all(sums.reshape(devices, 1, LANES), ('lat', 'lon'), 0, 0, til...  5.65 us
    pallas_call x1, Pallas kernels, local(): call(results_kernel, (f32(depth * rows, LANES), slab, slab), [IN_VMEM] *...  3.51 us
    ppermute x1, starting transfers between devices, local(): first = lax.ppermute(first, 'lat', [(i, i ^ 1) for i in range(lat_count)])  2.68 us
    pallas_call x1, Pallas kernels, local(): call(edges_kernel, (tile, tile), [IN_HBM] * 3, (IN_VMEM,) * 2, 2.0, [pltp...  1.59 us
    pallas_call x1, Pallas kernels, local(): call(functools.partial(own_kernel, lat_count), field, [IN_VMEM] * 4, IN_V...  1.52 us
  transfers between devices with their start and end apart: 3, of which 1 were waited for; matrix products, arithmetic and copies ran while one was open for 0% of the time, Pallas kernels for 10%

profile of v6, /device:TPU:1, one launch (start us, length us, event | category | flops | bytes accessed | tf_op | source)
XLA Modules:
  0.0 67.6 jit_solution(17369969781114126680)
XLA Ops:
  0.6 0.0 copy-start.5
  0.6 0.0 copy-start.2
  0.7 0.0 copy-start.1
  0.7 0.0 copy-start.3
  0.7 1.6 %shard_map.111 = (f32[8,4096]{1,0:T(8,128)S(1)}, f32[8,4096]{1,0:T(8,128)S(1)}) custom-call(f32[2,24,4096]{2,1,0:T(8,128)} %obs.7, f32[2,24,4096]{2,1,0:T(8,128)} %aux.5, f32[2,24,4096]{2,1,0:T(8,128)} %dual.7), custom_call_target="tpu_custom_call" | custom-call | flops 2000000000 | tf_op jit(solution)/shard_map/pallas_call | solution.py:325
  2.3 0.0 copy-start
  2.3 0.0 copy-start.4
  2.3 1.5 %collective-permute-start = (f32[8,4096]{1,0:T(8,128)S(1)}, f32[8,4096]{1,0:T(8,128)S(1)}, u32[]{:S(2)}, u32[]{:S(2)}) collective-permute-start(f32[8,4096]{1,0:T(8,128)S(1)} %get-tuple-element.14), channel_id=1, source_target_pairs={{0,1},{1,0},{2,3},{3,2},{4,5},{5,4},{6,7},{7,6},{8,9},{9,8},{10,11... | collective-permute-start | bytes 393224 | tf_op jit(solution)/shard_map/ppermute | solution.py:335
  3.8 2.7 %collective-permute-start.1 = (f32[8,4096]{1,0:T(8,128)S(1)}, f32[8,4096]{1,0:T(8,128)S(1)}, u32[]{:S(2)}, u32[]{:S(2)}) collective-permute-start(f32[8,4096]{1,0:T(8,128)S(1)} %get-tuple-element.15), channel_id=1, source_target_pairs={{0,32},{32,0},{64,96},{96,64},{1,33},{33,1},{65,97},{97,65},{2,34}... | collective-permute-start | bytes 393224 | tf_op jit(solution)/shard_map/ppermute | solution.py:334
  6.5 0.0 copy-done.5
  6.5 0.0 copy-done.2
  6.5 0.0 copy-done.1
  6.5 0.0 copy-done.3
  6.5 1.5 %shard_map.110.own = f32[32,2,24,128]{3,2,1,0:T(8,128)S(1)} custom-call(f32[2,24,4096]{2,1,0:T(8,128)S(1)} %copy-done.2, f32[2,24,4096]{2,1,0:T(8,128)S(1)} %copy-done.1, f32[2,24,4096]{2,1,0:T(8,128)S(1)} %copy-done.3, bf16[512,512]{1,0:T(8,128)(2,1)S(1)} %copy-done.5), custom_call_target="tpu_custom_call" | custom-call | flops 3000000000 | tf_op jit(solution)/shard_map/pallas_call | solution.py:336
  8.0 0.0 copy-done
  8.0 0.0 copy-done.4
  8.0 0.0 copy-start.6
  8.1 1.4 %shard_map.112 = (bf16[512,192]{1,0:T(8,128)(2,1)S(1)}, bf16[64,192]{1,0:T(8,128)(2,1)S(1)}) custom-call(f32[64,512]{1,0:T(8,128)S(1)} %copy-done.4, f32[512,512]{1,0:T(8,128)S(1)} %copy-done), custom_call_target="tpu_custom_call" | custom-call | flops 2000000000 | tf_op jit(solution)/shard_map/pallas_call | solution.py:339
  9.5 0.0 collective-permute-done.second
  9.5 0.0 collective-permute-done.1.first
  9.5 0.0 copy-done.6
  9.5 0.5 shard_map.113
  9.9 22.6 %all_to_all.15 = f32[32,2,24,128]{3,2,1,0:T(8,128)S(1)} all-to-all(f32[32,2,24,128]{3,2,1,0:T(8,128)S(1)} %shard_map.113), channel_id=1, replica_groups=mesh['lat'=4,'lon'=32] {'lon'}, dimensions={0} | all-to-all | bytes 1572864 | tf_op jit(solution)/shard_map/all_to_all | solution.py:349
  32.5 0.4 shard_map.114
  32.9 17.9 %all_to_all.16.fitted = f32[32,2,24,128]{3,2,1,0:T(8,128)S(1)} all-to-all(f32[32,2,24,128]{3,2,1,0:T(8,128)S(1)} %bitcast.11), channel_id=1, replica_groups=mesh['lat'=4,'lon'=32] {'lon'}, dimensions={0} | all-to-all | bytes 1572864 | tf_op jit(solution)/shard_map/all_to_all | solution.py:351
  50.7 1.0 %shard_map.115.after = f32[128,128]{1,0:T(8,128)} custom-call(f32[2,24,4096]{2,1,0:T(8,128)S(1)} %copy-done.2, f32[2,24,4096]{2,1,0:T(8,128)S(1)} %copy-done.1, f32[2,24,4096]{2,1,0:T(8,128)S(1)} %copy-done.3, f32[32,2,24,128]{3,2,1,0:T(8,128)S(1)} %all_to_all.16.fitted), custom_call_target="tpu_custom_call" | custom-call | flops 1000000000 | tf_op jit(solution)/shard_map/pallas_call | solution.py:353
  51.8 5.6 %all-to-all-start.2 = ((f32[128,1,128]{2,1,0:T(1,128)}), f32[128,1,128]{2,1,0:T(1,128)S(1)}, u32[]{:S(2)}, u32[]{:S(2)}) async-start(f32[128,1,128]{2,1,0:T(1,128)} %bitcast.4), calls=%async_computation.2 | async-start | bytes 131072 | tf_op jit(solution)/shard_map/all_to_all | solution.py:371
  57.4 3.5 %shard_map.116 = (f32[12288,128]{1,0:T(8,128)}, f32[2,24,4096]{2,1,0:T(8,128)}, f32[2,24,4096]{2,1,0:T(8,128)}) custom-call(f32[1536,128]{1,0:T(8,128)S(1)} %bitcast.10, bf16[512,192]{1,0:T(8,128)(2,1)S(1)} %get-tuple-element.17.matrix, f32[2,24,4096]{2,1,0:T(8,128)S(1)} %copy-done.2, f32[2,24,4096]{2,1,0:T(8,128)S(1)} %copy-done.3, ...), custom_call_target="tpu_custom_call" | custom-call | flops 5000000000 | tf_op jit(solution)/shard_map/pallas_call | solution.py:356
  60.9 6.1 %all-to-all-done.2 = f32[128,1,128]{2,1,0:T(1,128)S(1)} async-done(((f32[128,1,128]{2,1,0:T(1,128)}), f32[128,1,128]{2,1,0:T(1,128)S(1)}, u32[]{:S(2)}, u32[]{:S(2)}) %all-to-all-start.2) | async-done | bytes 65568 | tf_op jit(solution)/shard_map/all_to_all | solution.py:371
  67.0 0.6 shard_map.117
Async XLA Ops:
  0.6 5.8 %copy-start.5 = (bf16[512,512]{1,0:T(8,128)(2,1)S(1)}, bf16[512,512]{1,0:T(8,128)(2,1)}, u32[]{:S(2)}) copy-start(bf16[512,512]{1,0:T(8,128)(2,1)} %constant.4.clone.operator) | copy-start | bytes 1572868
  0.6 5.8 %copy-start.2 = (f32[2,24,4096]{2,1,0:T(8,128)S(1)}, f32[2,24,4096]{2,1,0:T(8,128)}, u32[]{:S(2)}) copy-start(f32[2,24,4096]{2,1,0:T(8,128)} %obs.7) | copy-start | bytes 2359300
  0.7 5.8 %copy-start.1 = (f32[2,24,4096]{2,1,0:T(8,128)S(1)}, f32[2,24,4096]{2,1,0:T(8,128)}, u32[]{:S(2)}) copy-start(f32[2,24,4096]{2,1,0:T(8,128)} %aux.5) | copy-start | bytes 2359300
  0.7 5.8 %copy-start.3 = (f32[2,24,4096]{2,1,0:T(8,128)S(1)}, f32[2,24,4096]{2,1,0:T(8,128)}, u32[]{:S(2)}) copy-start(f32[2,24,4096]{2,1,0:T(8,128)} %dual.7) | copy-start | bytes 2359300
  2.3 5.8 %copy-start = (f32[512,512]{1,0:T(8,128)S(1)}, f32[512,512]{1,0:T(8,128)}, u32[]{:S(2)}) copy-start(f32[512,512]{1,0:T(8,128)} %inverse_gram.1) | copy-start | bytes 3145732
  2.3 5.7 %copy-start.4 = (f32[64,512]{1,0:T(8,128)S(1)}, f32[64,512]{1,0:T(8,128)}, u32[]{:S(2)}) copy-start(f32[64,512]{1,0:T(8,128)} %predictors.1) | copy-start | bytes 393220
  2.3 7.2 %collective-permute-start = (f32[8,4096]{1,0:T(8,128)S(1)}, f32[8,4096]{1,0:T(8,128)S(1)}, u32[]{:S(2)}, u32[]{:S(2)}) collective-permute-start(f32[8,4096]{1,0:T(8,128)S(1)} %get-tuple-element.14), channel_id=1, source_target_pairs={{0,1},{1,0},{2,3},{3,2},{4,5},{5,4},{6,7},{7,6},{8,9},{9,8},{10,11... | collective-permute-start | bytes 393224 | tf_op jit(solution)/shard_map/ppermute | solution.py:335
  3.8 5.7 %collective-permute-start.1 = (f32[8,4096]{1,0:T(8,128)S(1)}, f32[8,4096]{1,0:T(8,128)S(1)}, u32[]{:S(2)}, u32[]{:S(2)}) collective-permute-start(f32[8,4096]{1,0:T(8,128)S(1)} %get-tuple-element.15), channel_id=1, source_target_pairs={{0,32},{32,0},{64,96},{96,64},{1,33},{33,1},{65,97},{97,65},{2,34}... | collective-permute-start | bytes 393224 | tf_op jit(solution)/shard_map/ppermute | solution.py:334
  8.0 1.4 %copy-start.6 = (bf16[512,384]{1,0:T(8,128)(2,1)S(1)}, bf16[512,384]{1,0:T(8,128)(2,1)}, u32[]{:S(2)}) copy-start(bf16[512,384]{1,0:T(8,128)(2,1)} %constant.5.clone.operator) | copy-start | bytes 1179652
  51.8 15.3 %all-to-all-start.2 = ((f32[128,1,128]{2,1,0:T(1,128)}), f32[128,1,128]{2,1,0:T(1,128)S(1)}, u32[]{:S(2)}, u32[]{:S(2)}) async-start(f32[128,1,128]{2,1,0:T(1,128)} %bitcast.4), calls=%async_computation.2 | async-start | bytes 131072 | tf_op jit(solution)/shard_map/all_to_all | solution.py:371

commit v7 on v6

--- a/solution.py
+++ b/solution.py
@@ -308,9 +308,10 @@
 
 def norms_kernel(sums, primal, change):
     row = jnp.sum(sums[...], axis=0, keepdims=True)
-    half = iota(row.shape, 1) < LANES // 2
-    primal[...] = jnp.sqrt(jnp.sum(jnp.where(half, row, 0.0), axis=1, keepdims=True))
-    change[...] = PENALTY * jnp.sqrt(jnp.sum(jnp.where(half, 0.0, row), axis=1, keepdims=True))
+    half = (iota((TILE, LANES), 1) < LANES // 2) == (iota((TILE, LANES), 0) == 0)
+    norms = jnp.sqrt(jnp.sum(jnp.where(half, row, 0.0), axis=1, keepdims=True))
+    primal[...] = norms[:1]
+    change[...] = PENALTY * norms[1:2]
 
 
 def local(lat_count, lon_count, observations, aux_state, dual_state, predictors, inverse_gram):

time: 67.9 us -> 67.9 us (level)
  no operation moved by 1% of the time
where the time goes in v7:
time: 67.9 us; the launch traced here: 67.6 us
  blocking collectives  40.4 us (59%)
  Pallas kernels  10.5 us (15%)
  starting transfers between devices  9.83 us (14%)
  waiting for transfers between devices  6.1 us (9%)
  between operations  0.77 us (1%)
    all_to_all x1, blocking collectives, local(): lax.all_to_all(smooth, 'lon', 0, 0, tiled=True)  22.6 us
    all_to_all x1, blocking collectives, local(): lax.all_to_all(fitted.reshape(field.shape), 'lon', 0, 0, tiled=True)  17.9 us
    all_to_all x1, waiting for transfers between devices, local(): lax.all_to_all(sums.reshape(devices, 1, LANES), ('lat', 'lon'), 0, 0, til...  6.09 us
    all_to_all x1, starting transfers between devices, local(): lax.all_to_all(sums.reshape(devices, 1, LANES), ('lat', 'lon'), 0, 0, til...  5.65 us
    pallas_call x1, Pallas kernels, local(): call(results_kernel, (f32(depth * rows, LANES), slab, slab), [IN_VMEM] *...  3.51 us
    ppermute x1, starting transfers between devices, local(): first = lax.ppermute(first, 'lat', [(i, i ^ 1) for i in range(lat_count)])  2.68 us
    pallas_call x1, Pallas kernels, local(): call(edges_kernel, (tile, tile), [IN_HBM] * 3, (IN_VMEM,) * 2, 2.0, [pltp...  1.59 us
    pallas_call x1, Pallas kernels, local(): call(functools.partial(own_kernel, lat_count), field, [IN_VMEM] * 4, IN_V...  1.52 us
  transfers between devices with their start and end apart: 3, of which 1 were waited for; matrix products, arithmetic and copies ran while one was open for 0% of the time, Pallas kernels for 10%

profile of v7, /device:TPU:1, one launch (start us, length us, event | category | flops | bytes accessed | tf_op | source)
XLA Modules:
  0.0 67.6 jit_solution(15794527587792596497)
XLA Ops:
  0.6 0.0 copy-start.5
  0.6 0.0 copy-start.2
  0.7 0.0 copy-start.1
  0.7 0.0 copy-start.3
  0.7 1.6 %shard_map.111 = (f32[8,4096]{1,0:T(8,128)S(1)}, f32[8,4096]{1,0:T(8,128)S(1)}) custom-call(f32[2,24,4096]{2,1,0:T(8,128)} %obs.7, f32[2,24,4096]{2,1,0:T(8,128)} %aux.5, f32[2,24,4096]{2,1,0:T(8,128)} %dual.7), custom_call_target="tpu_custom_call" | custom-call | flops 2000000000 | tf_op jit(solution)/shard_map/pallas_call | solution.py:326
  2.3 0.0 copy-start
  2.3 0.0 copy-start.4
  2.3 1.5 %collective-permute-start = (f32[8,4096]{1,0:T(8,128)S(1)}, f32[8,4096]{1,0:T(8,128)S(1)}, u32[]{:S(2)}, u32[]{:S(2)}) collective-permute-start(f32[8,4096]{1,0:T(8,128)S(1)} %get-tuple-element.14), channel_id=1, source_target_pairs={{0,1},{1,0},{2,3},{3,2},{4,5},{5,4},{6,7},{7,6},{8,9},{9,8},{10,11... | collective-permute-start | bytes 393224 | tf_op jit(solution)/shard_map/ppermute | solution.py:336
  3.8 2.7 %collective-permute-start.1 = (f32[8,4096]{1,0:T(8,128)S(1)}, f32[8,4096]{1,0:T(8,128)S(1)}, u32[]{:S(2)}, u32[]{:S(2)}) collective-permute-start(f32[8,4096]{1,0:T(8,128)S(1)} %get-tuple-element.15), channel_id=1, source_target_pairs={{0,32},{32,0},{64,96},{96,64},{1,33},{33,1},{65,97},{97,65},{2,34}... | collective-permute-start | bytes 393224 | tf_op jit(solution)/shard_map/ppermute | solution.py:335
  6.5 0.0 copy-done.5
  6.5 0.0 copy-done.2
  6.5 0.0 copy-done.1
  6.5 0.0 copy-done.3
  6.5 1.5 %shard_map.110.own = f32[32,2,24,128]{3,2,1,0:T(8,128)S(1)} custom-call(f32[2,24,4096]{2,1,0:T(8,128)S(1)} %copy-done.2, f32[2,24,4096]{2,1,0:T(8,128)S(1)} %copy-done.1, f32[2,24,4096]{2,1,0:T(8,128)S(1)} %copy-done.3, bf16[512,512]{1,0:T(8,128)(2,1)S(1)} %copy-done.5), custom_call_target="tpu_custom_call" | custom-call | flops 3000000000 | tf_op jit(solution)/shard_map/pallas_call | solution.py:337
  8.0 0.0 copy-done
  8.0 0.0 copy-done.4
  8.0 0.0 copy-start.6
  8.1 1.4 %shard_map.112 = (bf16[512,192]{1,0:T(8,128)(2,1)S(1)}, bf16[64,192]{1,0:T(8,128)(2,1)S(1)}) custom-call(f32[64,512]{1,0:T(8,128)S(1)} %copy-done.4, f32[512,512]{1,0:T(8,128)S(1)} %copy-done), custom_call_target="tpu_custom_call" | custom-call | flops 2000000000 | tf_op jit(solution)/shard_map/pallas_call | solution.py:340
  9.5 0.0 collective-permute-done.second
  9.5 0.0 collective-permute-done.1.first
  9.5 0.0 copy-done.6
  9.5 0.5 shard_map.113
  9.9 22.6 %all_to_all.15 = f32[32,2,24,128]{3,2,1,0:T(8,128)S(1)} all-to-all(f32[32,2,24,128]{3,2,1,0:T(8,128)S(1)} %shard_map.113), channel_id=1, replica_groups=mesh['lat'=4,'lon'=32] {'lon'}, dimensions={0} | all-to-all | bytes 1572864 | tf_op jit(solution)/shard_map/all_to_all | solution.py:350
  32.5 0.4 shard_map.114
  32.9 17.9 %all_to_all.16.fitted = f32[32,2,24,128]{3,2,1,0:T(8,128)S(1)} all-to-all(f32[32,2,24,128]{3,2,1,0:T(8,128)S(1)} %bitcast.11), channel_id=1, replica_groups=mesh['lat'=4,'lon'=32] {'lon'}, dimensions={0} | all-to-all | bytes 1572864 | tf_op jit(solution)/shard_map/all_to_all | solution.py:352
  50.7 1.0 %shard_map.115.after = f32[128,128]{1,0:T(8,128)} custom-call(f32[2,24,4096]{2,1,0:T(8,128)S(1)} %copy-done.2, f32[2,24,4096]{2,1,0:T(8,128)S(1)} %copy-done.1, f32[2,24,4096]{2,1,0:T(8,128)S(1)} %copy-done.3, f32[32,2,24,128]{3,2,1,0:T(8,128)S(1)} %all_to_all.16.fitted), custom_call_target="tpu_custom_call" | custom-call | flops 1000000000 | tf_op jit(solution)/shard_map/pallas_call | solution.py:354
  51.8 5.6 %all-to-all-start.2 = ((f32[128,1,128]{2,1,0:T(1,128)}), f32[128,1,128]{2,1,0:T(1,128)S(1)}, u32[]{:S(2)}, u32[]{:S(2)}) async-start(f32[128,1,128]{2,1,0:T(1,128)} %bitcast.4), calls=%async_computation.2 | async-start | bytes 131072 | tf_op jit(solution)/shard_map/all_to_all | solution.py:372
  57.4 3.5 %shard_map.116 = (f32[12288,128]{1,0:T(8,128)}, f32[2,24,4096]{2,1,0:T(8,128)}, f32[2,24,4096]{2,1,0:T(8,128)}) custom-call(f32[1536,128]{1,0:T(8,128)S(1)} %bitcast.10, bf16[512,192]{1,0:T(8,128)(2,1)S(1)} %get-tuple-element.17.matrix, f32[2,24,4096]{2,1,0:T(8,128)S(1)} %copy-done.2, f32[2,24,4096]{2,1,0:T(8,128)S(1)} %copy-done.3, ...), custom_call_target="tpu_custom_call" | custom-call | flops 5000000000 | tf_op jit(solution)/shard_map/pallas_call | solution.py:357
  60.9 6.1 %all-to-all-done.2 = f32[128,1,128]{2,1,0:T(1,128)S(1)} async-done(((f32[128,1,128]{2,1,0:T(1,128)}), f32[128,1,128]{2,1,0:T(1,128)S(1)}, u32[]{:S(2)}, u32[]{:S(2)}) %all-to-all-start.2) | async-done | bytes 65568 | tf_op jit(solution)/shard_map/all_to_all | solution.py:372
  67.0 0.6 shard_map.117
Async XLA Ops:
  0.6 5.8 %copy-start.5 = (bf16[512,512]{1,0:T(8,128)(2,1)S(1)}, bf16[512,512]{1,0:T(8,128)(2,1)}, u32[]{:S(2)}) copy-start(bf16[512,512]{1,0:T(8,128)(2,1)} %constant.4.clone.operator) | copy-start | bytes 1572868
  0.6 5.8 %copy-start.2 = (f32[2,24,4096]{2,1,0:T(8,128)S(1)}, f32[2,24,4096]{2,1,0:T(8,128)}, u32[]{:S(2)}) copy-start(f32[2,24,4096]{2,1,0:T(8,128)} %obs.7) | copy-start | bytes 2359300
  0.7 5.8 %copy-start.1 = (f32[2,24,4096]{2,1,0:T(8,128)S(1)}, f32[2,24,4096]{2,1,0:T(8,128)}, u32[]{:S(2)}) copy-start(f32[2,24,4096]{2,1,0:T(8,128)} %aux.5) | copy-start | bytes 2359300
  0.7 5.8 %copy-start.3 = (f32[2,24,4096]{2,1,0:T(8,128)S(1)}, f32[2,24,4096]{2,1,0:T(8,128)}, u32[]{:S(2)}) copy-start(f32[2,24,4096]{2,1,0:T(8,128)} %dual.7) | copy-start | bytes 2359300
  2.3 5.8 %copy-start = (f32[512,512]{1,0:T(8,128)S(1)}, f32[512,512]{1,0:T(8,128)}, u32[]{:S(2)}) copy-start(f32[512,512]{1,0:T(8,128)} %inverse_gram.1) | copy-start | bytes 3145732
  2.3 5.7 %copy-start.4 = (f32[64,512]{1,0:T(8,128)S(1)}, f32[64,512]{1,0:T(8,128)}, u32[]{:S(2)}) copy-start(f32[64,512]{1,0:T(8,128)} %predictors.1) | copy-start | bytes 393220
  2.3 7.2 %collective-permute-start = (f32[8,4096]{1,0:T(8,128)S(1)}, f32[8,4096]{1,0:T(8,128)S(1)}, u32[]{:S(2)}, u32[]{:S(2)}) collective-permute-start(f32[8,4096]{1,0:T(8,128)S(1)} %get-tuple-element.14), channel_id=1, source_target_pairs={{0,1},{1,0},{2,3},{3,2},{4,5},{5,4},{6,7},{7,6},{8,9},{9,8},{10,11... | collective-permute-start | bytes 393224 | tf_op jit(solution)/shard_map/ppermute | solution.py:336
  3.8 5.7 %collective-permute-start.1 = (f32[8,4096]{1,0:T(8,128)S(1)}, f32[8,4096]{1,0:T(8,128)S(1)}, u32[]{:S(2)}, u32[]{:S(2)}) collective-permute-start(f32[8,4096]{1,0:T(8,128)S(1)} %get-tuple-element.15), channel_id=1, source_target_pairs={{0,32},{32,0},{64,96},{96,64},{1,33},{33,1},{65,97},{97,65},{2,34}... | collective-permute-start | bytes 393224 | tf_op jit(solution)/shard_map/ppermute | solution.py:335
  8.0 1.4 %copy-start.6 = (bf16[512,384]{1,0:T(8,128)(2,1)S(1)}, bf16[512,384]{1,0:T(8,128)(2,1)}, u32[]{:S(2)}) copy-start(bf16[512,384]{1,0:T(8,128)(2,1)} %constant.5.clone.operator) | copy-start | bytes 1179652
  51.8 15.3 %all-to-all-start.2 = ((f32[128,1,128]{2,1,0:T(1,128)}), f32[128,1,128]{2,1,0:T(1,128)S(1)}, u32[]{:S(2)}, u32[]{:S(2)}) async-start(f32[128,1,128]{2,1,0:T(1,128)} %bitcast.4), calls=%async_computation.2 | async-start | bytes 131072 | tf_op jit(solution)/shard_map/all_to_all | solution.py:372

commit v8 on v6

--- a/solution.py
+++ b/solution.py
@@ -350,7 +350,7 @@
     fitted = call(fitted_kernel, f32(all_days * rows, LANES), [IN_VMEM] * 2, IN_VMEM, 2.0)(smooth, to_fitted)
     fitted = lax.all_to_all(fitted.reshape(field.shape), "lon", 0, 0, tiled=True)
     devices = lat_count * lon_count
-    sums = call(sums_kernel, f32(devices, LANES), [IN_VMEM] * 4, IN_VMEM, 1.0)(
+    sums = call(sums_kernel, f32(1, LANES), [IN_VMEM] * 4, IN_VMEM, 1.0)(
         *state, fitted
     )
     coefficients, aux_next, dual_next = call(
@@ -368,7 +368,8 @@
         ],
     )(smooth, to_coefficients, observations, dual_state, fitted, sums)
     coefficients = coefficients.reshape(depth, rows, LANES)
-    sums = lax.all_to_all(sums.reshape(devices, 1, LANES), ("lat", "lon"), 0, 0, tiled=True).reshape(devices, LANES)
+    sums = jnp.broadcast_to(sums[None], (devices, 1, LANES))
+    sums = lax.all_to_all(sums, ("lat", "lon"), 0, 0, tiled=True).reshape(devices, LANES)
     primal, change = call(norms_kernel, (f32(1, 1), f32(1, 1)), [IN_VMEM], (IN_VMEM, IN_VMEM), 0.5)(sums)
     return (coefficients, aux_next, dual_next, primal.reshape(()), change.reshape(()))
 

time: 67.9 us -> 67.9 us (level)
  no operation moved by 1% of the time
where the time goes in v8:
time: 67.9 us; the launch traced here: 67.7 us
  blocking collectives  40.4 us (59%)
  Pallas kernels  9.89 us (15%)
  starting transfers between devices  9.83 us (14%)
  waiting for transfers between devices  6.09 us (9%)
  between operations  0.77 us (1%)
  local copies, waits for them, and re-layouts  0.69 us (1%)
    all_to_all x1, blocking collectives, local(): lax.all_to_all(smooth, 'lon', 0, 0, tiled=True)  22.5 us
    all_to_all x1, blocking collectives, local(): lax.all_to_all(fitted.reshape(field.shape), 'lon', 0, 0, tiled=True)  17.9 us
    all_to_all x1, waiting for transfers between devices, local(): lax.all_to_all(sums, ('lat', 'lon'), 0, 0, tiled=True)  6.09 us
    all_to_all x1, starting transfers between devices, local(): lax.all_to_all(sums, ('lat', 'lon'), 0, 0, tiled=True)  5.65 us
    pallas_call x1, Pallas kernels, local(): call(results_kernel, (f32(depth * rows, LANES), slab, slab), [IN_VMEM] *...  3.51 us
    ppermute x1, starting transfers between devices, local(): first = lax.ppermute(first, 'lat', [(i, i ^ 1) for i in range(lat_count)])  2.68 us
    pallas_call x1, Pallas kernels, local(): call(edges_kernel, (tile, tile), [IN_HBM] * 3, (IN_VMEM,) * 2, 2.0, [pltp...  1.59 us
    pallas_call x1, Pallas kernels, local(): call(functools.partial(own_kernel, lat_count), field, [IN_VMEM] * 4, IN_V...  1.54 us
  transfers between devices with their start and end apart: 3, of which 1 were waited for; matrix products, arithmetic and copies ran while one was open for 0% of the time, Pallas kernels for 10%

profile of v8, /device:TPU:1, one launch (start us, length us, event | category | flops | bytes accessed | tf_op | source)
XLA Modules:
  0.0 67.7 jit_solution(5117693542459776661)
XLA Ops:
  0.6 0.0 copy-start.5
  0.6 0.0 copy-start.2
  0.7 0.0 copy-start.1
  0.7 0.0 copy-start.3
  0.7 1.6 %shard_map.111 = (f32[8,4096]{1,0:T(8,128)S(1)}, f32[8,4096]{1,0:T(8,128)S(1)}) custom-call(f32[2,24,4096]{2,1,0:T(8,128)} %obs.7, f32[2,24,4096]{2,1,0:T(8,128)} %aux.5, f32[2,24,4096]{2,1,0:T(8,128)} %dual.7), custom_call_target="tpu_custom_call" | custom-call | flops 2000000000 | tf_op jit(solution)/shard_map/pallas_call | solution.py:325
  2.3 0.0 copy-start
  2.3 0.0 copy-start.4
  2.3 1.5 %collective-permute-start = (f32[8,4096]{1,0:T(8,128)S(1)}, f32[8,4096]{1,0:T(8,128)S(1)}, u32[]{:S(2)}, u32[]{:S(2)}) collective-permute-start(f32[8,4096]{1,0:T(8,128)S(1)} %get-tuple-element.14), channel_id=1, source_target_pairs={{0,1},{1,0},{2,3},{3,2},{4,5},{5,4},{6,7},{7,6},{8,9},{9,8},{10,11... | collective-permute-start | bytes 393224 | tf_op jit(solution)/shard_map/ppermute | solution.py:335
  3.8 2.7 %collective-permute-start.1 = (f32[8,4096]{1,0:T(8,128)S(1)}, f32[8,4096]{1,0:T(8,128)S(1)}, u32[]{:S(2)}, u32[]{:S(2)}) collective-permute-start(f32[8,4096]{1,0:T(8,128)S(1)} %get-tuple-element.15), channel_id=1, source_target_pairs={{0,32},{32,0},{64,96},{96,64},{1,33},{33,1},{65,97},{97,65},{2,34}... | collective-permute-start | bytes 393224 | tf_op jit(solution)/shard_map/ppermute | solution.py:334
  6.5 0.0 copy-done.5
  6.5 0.0 copy-done.2
  6.5 0.0 copy-done.1
  6.5 0.0 copy-done.3
  6.5 1.5 %shard_map.110.own = f32[32,2,24,128]{3,2,1,0:T(8,128)S(1)} custom-call(f32[2,24,4096]{2,1,0:T(8,128)S(1)} %copy-done.2, f32[2,24,4096]{2,1,0:T(8,128)S(1)} %copy-done.1, f32[2,24,4096]{2,1,0:T(8,128)S(1)} %copy-done.3, bf16[512,512]{1,0:T(8,128)(2,1)S(1)} %copy-done.5), custom_call_target="tpu_custom_call" | custom-call | flops 3000000000 | tf_op jit(solution)/shard_map/pallas_call | solution.py:336
  8.0 0.0 copy-done
  8.1 0.0 copy-done.4
  8.1 0.0 copy-start.6
  8.1 1.4 %shard_map.112 = (bf16[512,192]{1,0:T(8,128)(2,1)S(1)}, bf16[64,192]{1,0:T(8,128)(2,1)S(1)}) custom-call(f32[64,512]{1,0:T(8,128)S(1)} %copy-done.4, f32[512,512]{1,0:T(8,128)S(1)} %copy-done), custom_call_target="tpu_custom_call" | custom-call | flops 2000000000 | tf_op jit(solution)/shard_map/pallas_call | solution.py:339
  9.5 0.0 collective-permute-done.second
  9.5 0.0 collective-permute-done.1.first
  9.5 0.0 copy-done.6
  9.5 0.5 shard_map.113
  10.0 22.5 %all_to_all.15 = f32[32,2,24,128]{3,2,1,0:T(8,128)S(1)} all-to-all(f32[32,2,24,128]{3,2,1,0:T(8,128)S(1)} %shard_map.113), channel_id=1, replica_groups=mesh['lat'=4,'lon'=32] {'lon'}, dimensions={0} | all-to-all | bytes 1572864 | tf_op jit(solution)/shard_map/all_to_all | solution.py:349
  32.5 0.4 shard_map.114
  32.9 17.9 %all_to_all.16.fitted = f32[32,2,24,128]{3,2,1,0:T(8,128)S(1)} all-to-all(f32[32,2,24,128]{3,2,1,0:T(8,128)S(1)} %bitcast.9), channel_id=1, replica_groups=mesh['lat'=4,'lon'=32] {'lon'}, dimensions={0} | all-to-all | bytes 1572864 | tf_op jit(solution)/shard_map/all_to_all | solution.py:351
  50.7 0.4 shard_map.115.after
  51.2 0.7 broadcast_in_dim.9
  51.8 5.6 %all-to-all-start.2 = ((f32[128,1,128]{2,1,0:T(1,128)}), f32[128,1,128]{2,1,0:T(1,128)S(1)}, u32[]{:S(2)}, u32[]{:S(2)}) async-start(f32[128,1,128]{2,1,0:T(1,128)} %broadcast_in_dim.9), calls=%async_computation.2 | async-start | bytes 131072 | tf_op jit(solution)/shard_map/all_to_all | solution.py:372
  57.5 3.5 %shard_map.116 = (f32[12288,128]{1,0:T(8,128)}, f32[2,24,4096]{2,1,0:T(8,128)}, f32[2,24,4096]{2,1,0:T(8,128)}) custom-call(f32[1536,128]{1,0:T(8,128)S(1)} %bitcast.8, bf16[512,192]{1,0:T(8,128)(2,1)S(1)} %get-tuple-element.17.matrix, f32[2,24,4096]{2,1,0:T(8,128)S(1)} %copy-done.2, f32[2,24,4096]{2,1,0:T(8,128)S(1)} %copy-done.3, ...), custom_call_target="tpu_custom_call" | custom-call | flops 5000000000 | tf_op jit(solution)/shard_map/pallas_call | solution.py:356
  61.0 6.1 %all-to-all-done.2 = f32[128,1,128]{2,1,0:T(1,128)S(1)} async-done(((f32[128,1,128]{2,1,0:T(1,128)}), f32[128,1,128]{2,1,0:T(1,128)S(1)}, u32[]{:S(2)}, u32[]{:S(2)}) %all-to-all-start.2) | async-done | bytes 65568 | tf_op jit(solution)/shard_map/all_to_all | solution.py:372
  67.1 0.6 shard_map.117
Async XLA Ops:
  0.6 5.8 %copy-start.5 = (bf16[512,512]{1,0:T(8,128)(2,1)S(1)}, bf16[512,512]{1,0:T(8,128)(2,1)}, u32[]{:S(2)}) copy-start(bf16[512,512]{1,0:T(8,128)(2,1)} %constant.4.clone.operator) | copy-start | bytes 1572868
  0.6 5.8 %copy-start.2 = (f32[2,24,4096]{2,1,0:T(8,128)S(1)}, f32[2,24,4096]{2,1,0:T(8,128)}, u32[]{:S(2)}) copy-start(f32[2,24,4096]{2,1,0:T(8,128)} %obs.7) | copy-start | bytes 2359300
  0.7 5.8 %copy-start.1 = (f32[2,24,4096]{2,1,0:T(8,128)S(1)}, f32[2,24,4096]{2,1,0:T(8,128)}, u32[]{:S(2)}) copy-start(f32[2,24,4096]{2,1,0:T(8,128)} %aux.5) | copy-start | bytes 2359300
  0.7 5.8 %copy-start.3 = (f32[2,24,4096]{2,1,0:T(8,128)S(1)}, f32[2,24,4096]{2,1,0:T(8,128)}, u32[]{:S(2)}) copy-start(f32[2,24,4096]{2,1,0:T(8,128)} %dual.7) | copy-start | bytes 2359300
  2.3 5.8 %copy-start = (f32[512,512]{1,0:T(8,128)S(1)}, f32[512,512]{1,0:T(8,128)}, u32[]{:S(2)}) copy-start(f32[512,512]{1,0:T(8,128)} %inverse_gram.1) | copy-start | bytes 3145732
  2.3 5.8 %copy-start.4 = (f32[64,512]{1,0:T(8,128)S(1)}, f32[64,512]{1,0:T(8,128)}, u32[]{:S(2)}) copy-start(f32[64,512]{1,0:T(8,128)} %predictors.1) | copy-start | bytes 393220
  2.3 7.2 %collective-permute-start = (f32[8,4096]{1,0:T(8,128)S(1)}, f32[8,4096]{1,0:T(8,128)S(1)}, u32[]{:S(2)}, u32[]{:S(2)}) collective-permute-start(f32[8,4096]{1,0:T(8,128)S(1)} %get-tuple-element.14), channel_id=1, source_target_pairs={{0,1},{1,0},{2,3},{3,2},{4,5},{5,4},{6,7},{7,6},{8,9},{9,8},{10,11... | collective-permute-start | bytes 393224 | tf_op jit(solution)/shard_map/ppermute | solution.py:335
  3.8 5.7 %collective-permute-start.1 = (f32[8,4096]{1,0:T(8,128)S(1)}, f32[8,4096]{1,0:T(8,128)S(1)}, u32[]{:S(2)}, u32[]{:S(2)}) collective-permute-start(f32[8,4096]{1,0:T(8,128)S(1)} %get-tuple-element.15), channel_id=1, source_target_pairs={{0,32},{32,0},{64,96},{96,64},{1,33},{33,1},{65,97},{97,65},{2,34}... | collective-permute-start | bytes 393224 | tf_op jit(solution)/shard_map/ppermute | solution.py:334
  8.1 1.4 %copy-start.6 = (bf16[512,384]{1,0:T(8,128)(2,1)S(1)}, bf16[512,384]{1,0:T(8,128)(2,1)}, u32[]{:S(2)}) copy-start(bf16[512,384]{1,0:T(8,128)(2,1)} %constant.5.clone.operator) | copy-start | bytes 1179652
  51.8 15.3 %all-to-all-start.2 = ((f32[128,1,128]{2,1,0:T(1,128)}), f32[128,1,128]{2,1,0:T(1,128)S(1)}, u32[]{:S(2)}, u32[]{:S(2)}) async-start(f32[128,1,128]{2,1,0:T(1,128)} %broadcast_in_dim.9), calls=%async_computation.2 | async-start | bytes 131072 | tf_op jit(solution)/shard_map/all_to_all | solution.py:372
